TPU v7x, 512 devices: a whole 4x4x16 slice. The times are simulated.
512 devices in a mesh: row: 16 (over z), col: 32 (over x, y, core).
Axes of the slice: x: 4, y: 4, z: 16, core: 2. Of those that a mesh axis runs over, the one named last changes fastest.
Arguments:
- slab: bfloat16 [12288, 65536], P('row', 'col'), may hold values from -6 to 6
- sketch: bfloat16 [65536, 256], P('col'), may hold values from -0.0234375 to 0.0234375
Outputs:
- basis: float32 [12288, 256], P(('row', 'col'))
- projected: float32 [256, 65536], P('row', 'col')
All inputs are finite; a program needn't handle non-finite values.
Results may differ from a plain program's by a relative error of at most 0.0027.
Values may be sent and summed in bfloat16 or wider, within the bound.
No kernel may reach another device: no remote copies, remote signals or barrier semaphores. Data moves between devices by JAX's collectives and lax.ppermute only.
A program may use at most 64 MiB of HBM per device.

v0:
```python
import jax
import jax.numpy as jnp
from jax import lax
from jax.sharding import PartitionSpec as P


def orthonormal(sampled, gram):
    lower = jnp.linalg.cholesky(gram)
    return jax.scipy.linalg.solve_triangular(lower, sampled.T, lower=True).T


def gram_of(sampled):
    return jnp.dot(
        sampled.T, sampled, precision=lax.Precision.HIGHEST, preferred_element_type=jnp.float32
    )


def local(slab, sketch):
    row_count = slab.shape[0]
    col_size = lax.axis_size("col")
    share_rows = row_count // col_size
    partial_sample = jnp.dot(slab, sketch, preferred_element_type=jnp.float32)
    sampled = lax.psum(partial_sample, "col")
    gram = lax.psum(gram_of(sampled), "row")
    full_basis = orthonormal(sampled, gram)
    basis = lax.dynamic_slice_in_dim(full_basis, lax.axis_index("col") * share_rows, share_rows, 0)
    basis_half = full_basis.astype(jnp.bfloat16)
    out_rows = basis_half.shape[1] // lax.axis_size("row")
    partial_proj = lax.dot_general(
        basis_half, slab, (((0,), (0,)), ((), ())), preferred_element_type=jnp.float32
    )
    summed = lax.psum(partial_proj, "row")
    projected = lax.dynamic_slice_in_dim(summed, lax.axis_index("row") * out_rows, out_rows, 0)
    return (basis, projected)


def solution(mesh):
    return jax.shard_map(
        local,
        mesh=mesh,
        in_specs=(P("row", "col"), P("col", None)),
        out_specs=(P(("row", "col"), None), P("row", "col")),
        check_vma=False,
    )
```

profile of v0, /device:TPU:6, one launch (start us, length us, event | category | flops | bytes accessed | tf_op | source)
XLA Modules:
  0.0 514.9 jit_solution(7883438454806041874)
XLA Ops:
  7.2 0.0 copy-start
  7.2 0.0 all-reduce.5.cloned.1.call-start
  7.2 1.8 copy-done
  9.1 3.1 fusion.15
  12.2 0.0 all-reduce.5.cloned.1.call-update
  12.2 0.0 all-reduce.7.cloned.1.call-start
  12.2 139.8 %all-reduce.5.cloned.1.call-done = f32[768,256]{1,0:T(8,128)} async-done(((f32[768,256]{1,0:T(8,128)}), f32[768,256]{1,0:T(8,128)}) %all-reduce.5.cloned.1.call-update) | async-done | bytes 786448 | tf_op jit(solution)/shard_map/psum | solution.py:23
  152.1 3.5 fusion.16
  155.6 0.0 all-reduce.7.cloned.1.call-update
  155.6 0.2 all-reduce.9.cloned.1.call-start
  155.9 134.2 %all-reduce.7.cloned.1.call-done = f32[256,256]{0,1:T(8,128)} async-done(((f32[256,256]{0,1:T(8,128)}), f32[256,256]{0,1:T(8,128)}) %all-reduce.7.cloned.1.call-update) | async-done | bytes 262160 | tf_op jit(solution)/shard_map/psum | solution.py:24
  290.1 1.1 copy.5
  291.2 1.0 fusion.5
  292.2 0.0 copy-start.4
  292.2 0.7 copy-done.4
  292.9 11.7 %cholesky.50 = f32[128,128]{1,0:T(8,128)S(1)} custom-call(f32[128,128]{1,0:T(8,128)S(1)} %cholesky.118), custom_call_target="Cholesky" | custom-call | tf_op jit(solution)/shard_map/jit(cholesky)/cholesky | solution.py:8
  304.6 9.8 %custom-call.15 = f32[1,128,128]{1,2,0:T(8,128)S(1)} custom-call(f32[1,128,128]{2,1,0:T(8,128)S(1)} %get-tuple-element.25), custom_call_target="InvertDiagBlocksLowerTriangular" | custom-call | tf_op jit(solution)/shard_map/jit(cholesky)/cholesky | solution.py:8
  314.5 1.0 constant_dynamic-update-slice_fusion
  315.5 1.1 convolution_subtract_fusion.1
  316.6 11.7 %cholesky.105 = f32[128,128]{1,0:T(8,128)S(1)} custom-call(f32[128,128]{1,0:T(8,128)S(1)} %convolution_subtract_fusion.1), custom_call_target="Cholesky" | custom-call | tf_op jit(solution)/shard_map/jit(cholesky)/cholesky | solution.py:8
  328.4 0.0 copy-start.3
  328.4 0.7 compare_reduce_fusion
  330.4 0.0 copy-done.3
  330.4 1.0 select_select_fusion
  331.4 0.1 triangular_solve.57
  331.4 5.3 %while.1 = (s32[]{:T(128)}, f32[256,256]{1,0:T(8,128)S(1)}, s32[2,2]{1,0:T(2,128)S(1)}, f32[2,128,128]{2,1,0:T(8,128)}, s32[]{:T(128)}) while((s32[]{:T(128)}, f32[256,256]{1,0:T(8,128)S(1)}, s32[2,2]{1,0:T(2,128)S(1)}, f32[2,128,128]{2,1,0:T(8,128)}, s32[]{:T(128)}) %tuple.28), condition=%wide.while_cond, body=%wide.while_body.sunk | while | flops 2 | bytes 132205 | solution.py:9
  331.6 0.6 fusion.27
  332.3 1.9 bitcast_dynamic-update-slice_fusion.2
  334.2 0.6 fusion.27
  334.8 1.9 bitcast_dynamic-update-slice_fusion.2
  336.7 0.0 copy-start.2
  336.7 21.1 %custom-call.16 = f32[2,128,128]{1,2,0:T(8,128)} custom-call(f32[2,128,128]{2,1,0:T(8,128)} %get-tuple-element.9), custom_call_target="InvertDiagBlocksLowerTriangular" | custom-call | tf_op jit(solution)/shard_map/jit(_solve_triangular)/triangular_solve | solution.py:9
  357.9 0.0 copy-done.2
  357.9 1.5 fusion.3
  359.4 1.8 convolution_subtract_fusion
  361.3 1.4 fusion.9
  362.6 0.0 copy-start.1
  362.6 0.7 copy-done.1
  363.4 2.3 fusion.1
  365.7 0.0 all-reduce.9.cloned.1.call-update
  365.7 1.7 fusion.7
  367.4 1.6 copy.6
  369.0 137.9 %all-reduce.9.cloned.1.call-done = f32[256,2048]{1,0:T(8,128)} async-done(((f32[256,2048]{1,0:T(8,128)}), f32[256,2048]{1,0:T(8,128)}) %all-reduce.9.cloned.1.call-update) | async-done | bytes 2097168 | tf_op jit(solution)/shard_map/psum | solution.py:32
  506.8 1.6 constant_dynamic-slice_fusion.1
  (8 shorter events, 0.1 us)
Async XLA Ops:
  7.2 1.9 copy-start
  7.2 144.9 %all-reduce.5.cloned.1.call-start = ((), (), s32[]{:S(2)}) async-start(), calls=%async_computation | async-start | bytes 1572864 | tf_op jit(solution)/shard_map/psum | solution.py:23
  12.2 277.9 %all-reduce.7.cloned.1.call-start = ((), (), s32[]{:S(2)}) async-start(), calls=%async_computation.1 | async-start | bytes 524288 | tf_op jit(solution)/shard_map/psum | solution.py:24
  155.6 351.2 %all-reduce.9.cloned.1.call-start = ((), (), s32[]{:S(2)}) async-start(), calls=%async_computation.2 | async-start | bytes 4194304 | tf_op jit(solution)/shard_map/psum | solution.py:32
  292.2 0.7 copy-start.4
  328.4 2.0 copy-start.3
  336.7 21.1 %copy-start.2 = (f32[256,256]{1,0:T(8,128)}, f32[256,256]{1,0:T(8,128)S(1)}, u32[]{:S(2)}) copy-start(f32[256,256]{1,0:T(8,128)S(1)} %get-tuple-element.80) | copy-start | bytes 786436
  362.6 0.8 copy-start.1
Sparse Core Ops, SparseCore 0:
  12.3 139.7 all-reduce.4
  155.7 134.3 all-reduce.6
  365.8 140.9 all-reduce.8
where the time goes:
time: 516 us; the launch traced here: 515 us
  waiting for transfers between devices  412 us (80%)
  other arithmetic  58.8 us (11%)
  matrix products  15.8 us (3%)
  between operations  15.1 us (3%)
  local copies, waits for them, and re-layouts  12.7 us (2%)
    psum x1, waiting for transfers between devices, local(): sampled = lax.psum(partial_sample, 'col')  140 us
    psum x1, waiting for transfers between devices, local(): summed = lax.psum(partial_proj, 'row')  138 us
    psum x1, waiting for transfers between devices, local(): gram = lax.psum(gram_of(sampled), 'row')  134 us
    another operation x6, other arithmetic, orthonormal(): lower = jnp.linalg.cholesky(gram)  34 us
    another operation x3, other arithmetic, orthonormal(): return jax.scipy.linalg.solve_triangular(lower, sampled.T, lower=True).T  22.1 us
  transfers between devices with their start and end apart: 3, of which 3 were waited for; matrix products, arithmetic and copies ran while one was open for 1% of the time, Pallas kernels for 0%

commit v1 on v0

v1 whole, which is shorter than its diff:
```python
import jax
import jax.numpy as jnp
from jax import lax
from jax.experimental import pallas as pl
from jax.experimental.pallas import tpu as pltpu
from jax.sharding import PartitionSpec as P

F32 = jnp.float32
F16 = jnp.float16
BF16 = jnp.bfloat16
EXACT = lax.Precision.HIGHEST
TILE = 64
GROUP = 4
SKETCH_SCALE = 128.0
SAMPLE_SCALE = 4.0
PROJ_SCALE = 128.0


def eliminate(tile, out_ref, n):
    groups = [tile[8 * g : 8 * g + 8, :] for g in range(n // 8)]
    shape = groups[0].shape
    sub = lax.broadcasted_iota(jnp.int32, shape, 0)
    for j in range(0, n, 2):
        g, s = j // 8, j % 8
        r0 = jnp.broadcast_to(groups[g][s : s + 1, :], shape)
        r1 = jnp.broadcast_to(groups[g][s + 1 : s + 2, :], shape)
        a = jnp.broadcast_to(r0[:, j : j + 1], shape)
        b = jnp.broadcast_to(r0[:, j + 1 : j + 2], shape)
        c = jnp.broadcast_to(r1[:, j + 1 : j + 2], shape)
        det = a * c - b * b
        inv = 1.0 / det
        ca, cb, cc = a * inv, b * inv, c * inv
        for h in range(g, n // 8):
            if h == g and s == 6:
                continue
            c0 = jnp.broadcast_to(groups[h][:, j : j + 1], shape)
            c1 = jnp.broadcast_to(groups[h][:, j + 1 : j + 2], shape)
            m0 = cc * c0 - cb * c1
            m1 = ca * c1 - cb * c0
            if h == g:
                live = sub > s + 1
                m0 = jnp.where(live, m0, 0.0)
                m1 = jnp.where(live, m1, 0.0)
            groups[h] = groups[h] - m0 * r0 - m1 * r1
        inv_a = 1.0 / a
        x0 = r0 * lax.rsqrt(a)
        x1 = (r1 - (b * inv_a) * r0) * lax.rsqrt(det * inv_a)
        out_ref[j : j + 1, :] = x0[0:1, :]
        out_ref[j + 1 : j + 2, :] = x1[0:1, :]


def inverse_factor_kernel(gram_ref, out_ref, aug, x_ref):
    n = gram_ref.shape[0]

    def eye(size):
        rows = lax.broadcasted_iota(jnp.int32, (size, size), 0)
        return (rows == lax.broadcasted_iota(jnp.int32, (size, size), 1)).astype(F32)

    aug[:, :n] = gram_ref[...]
    aug[:, n:] = eye(n)
    for k in range(n // TILE):
        lo, hi = k * TILE, (k + 1) * TILE
        tile = jnp.concatenate([aug[lo:hi, lo:hi], eye(TILE)], axis=1)
        eliminate(tile, x_ref, TILE)
        row = jnp.dot(x_ref[:, TILE:], aug[lo:hi, :], precision=EXACT, preferred_element_type=F32)
        out_ref[lo:hi, :] = row[:, n:]
        if hi < n:
            aug[hi:, :] = aug[hi:, :] - lax.dot_general(
                row[:, hi:n], row, (((0,), (0,)), ((), ())), precision=EXACT, preferred_element_type=F32
            )


def inverse_factor(gram):
    n = gram.shape[0]
    return pl.pallas_call(
        inverse_factor_kernel,
        out_shape=jax.ShapeDtypeStruct((n, n), F32),
        scratch_shapes=[pltpu.VMEM((n, 2 * n), F32), pltpu.VMEM((TILE, 2 * TILE), F32)],
        name="inverse_factor",
    )(gram)


def copies(x, count):
    return jnp.broadcast_to(x[None], (count, *x.shape))


def local(slab, sketch):
    rows, cols = slab.shape
    width = sketch.shape[1]
    col_size, row_size = lax.axis_size("col"), lax.axis_size("row")
    share = rows // col_size
    piece = width // col_size
    out_rows = width // row_size
    neighbours = [list(range(at, at + GROUP)) for at in range(0, row_size, GROUP)]
    with jax.named_scope("sample"):
        partial = jnp.dot(slab, sketch, preferred_element_type=F32)
        sent = (partial * SKETCH_SCALE).astype(F16).reshape(col_size, share, width)
        got = lax.all_to_all(sent, "col", 0, 0)
        own = jnp.sum(got.astype(F32), axis=0) * (1.0 / SKETCH_SCALE)
        shares = lax.all_to_all(copies((own * SAMPLE_SCALE).astype(F16), col_size), "col", 0, 0)
        sampled = shares.reshape(rows, width).astype(F32) * (1.0 / SAMPLE_SCALE)
    with jax.named_scope("gram"):
        part = lax.dot_general(sampled, sampled, (((0,), (0,)), ((), ())), precision=EXACT, preferred_element_type=F32)
        part = lax.dynamic_slice_in_dim(part, lax.axis_index("col") * piece, piece, 0)
        strip = jnp.sum(lax.all_to_all(copies(part, row_size), "row", 0, 0), axis=0)
        gram = lax.all_to_all(copies(strip, col_size), "col", 0, 0).reshape(width, width)
    with jax.named_scope("product"):
        high = sampled.astype(BF16)
        low = (sampled - high.astype(F32)).astype(BF16)
        product = lax.dot_general(high, slab, (((0,), (0,)), ((), ())), preferred_element_type=F32)
        product = product + lax.dot_general(low, slab, (((0,), (0,)), ((), ())), preferred_element_type=F32)
        product = product.reshape(width, GROUP, cols // GROUP).transpose(1, 0, 2)
        product = jnp.sum(lax.all_to_all(product, "row", 0, 0, axis_index_groups=neighbours), axis=0)
    with jax.named_scope("factor"):
        inverse = inverse_factor(gram)
    with jax.named_scope("basis"):
        basis = lax.dot_general(own, inverse, (((1,), (1,)), ((), ())), precision=EXACT, preferred_element_type=F32)
    with jax.named_scope("projected"):
        mine = jnp.dot(inverse, product, precision=EXACT, preferred_element_type=F32)
        sent = (mine * PROJ_SCALE).astype(F16).reshape(row_size, out_rows, cols // GROUP)
        got = lax.all_to_all(sent, "row", 0, 0).reshape(row_size // GROUP, GROUP, out_rows, cols // GROUP)
        projected = jnp.sum(got.astype(F32), axis=0) * (1.0 / PROJ_SCALE)
        projected = projected.transpose(1, 0, 2).reshape(out_rows, cols)
    return (basis, projected)


def solution(mesh):
    return jax.shard_map(
        local,
        mesh=mesh,
        in_specs=(P("row", "col"), P("col", None)),
        out_specs=(P(("row", "col"), None), P("row", "col")),
        check_vma=False,
    )
```

time: 516 us -> 169 us (0.33)
  waiting for transfers between devices: 412 us -> 66.8 us
  other arithmetic: 58.8 us -> 4.86 us
  starting transfers between devices: 0.3 us -> 36.5 us
  Pallas kernels: 0 us -> 21.6 us
  blocking collectives: 0 us -> 16.7 us
  between operations: 15.1 us -> 0.79 us
  local copies, waits for them, and re-layouts: 12.7 us -> 7.31 us
    psum x3 -> x0, waiting for transfers between devices: 412 us -> none  [the longest x1 140 us: local(): sampled = lax.psum(partial_sample, 'col')]
    all_to_all x0 -> x5, waiting for transfers between devices: none -> 66.8 us  [the longest x1 27.5 us: local(): lax.all_to_all(product, 'row', 0, 0, axis_index_groups=neighbours)]
    another operation x9 -> x0, other arithmetic: 56.1 us -> none  [the longest x6 34 us: orthonormal(): lower = jnp.linalg.cholesky(gram)]
    all_to_all x0 -> x5, starting transfers between devices: none -> 36.5 us  [the longest x1 14 us: local(): strip = jnp.sum(lax.all_to_all(copies(part, row_size), 'row', 0, 0), axis=0)]
    pallas_call x0 -> x1, Pallas kernels: none -> 21.6 us  [inverse_factor(): pl.pallas_call(inverse_factor_kernel, out_shape=jax.ShapeDtypeStruct((n,...]
    all_to_all x0 -> x1, blocking collectives: none -> 16.7 us  [local(): got = lax.all_to_all(sent, 'col', 0, 0)]
    another operation x5 -> x0, matrix products: 6.88 us -> none  [the longest x3 4.74 us: orthonormal(): return jax.scipy.linalg.solve_triangular(lower, sampled.T, lower=True).T]
    another operation x9 -> x0, local copies, waits for them, and re-layouts: 5.21 us -> none
  transfers between devices with their start and end apart: 3 -> 5, of which waited for: 3 -> 5; matrix products, arithmetic and copies ran while one was open for 1% -> 5% of each run, Pallas kernels for 0% -> 13%
where the time goes in v1:
time: 169 us; the launch traced here: 166 us
  waiting for transfers between devices  66.8 us (40%)
  starting transfers between devices  36.5 us (22%)
  Pallas kernels  21.6 us (13%)
  blocking collectives  16.7 us (10%)
  matrix products  12 us (7%)
  local copies, waits for them, and re-layouts  7.31 us (4%)
  other arithmetic  4.86 us (3%)
    all_to_all x1, waiting for transfers between devices, local(): lax.all_to_all(product, 'row', 0, 0, axis_index_groups=neighbours)  27.5 us
    pallas_call x1, Pallas kernels, inverse_factor(): pl.pallas_call(inverse_factor_kernel, out_shape=jax.ShapeDtypeStruct((n,...  21.6 us
    all_to_all x1, waiting for transfers between devices, local(): lax.all_to_all(sent, 'row', 0, 0)  17.2 us
    all_to_all x1, blocking collectives, local(): got = lax.all_to_all(sent, 'col', 0, 0)  16.7 us
    all_to_all x1, starting transfers between devices, local(): strip = jnp.sum(lax.all_to_all(copies(part, row_size), 'row', 0, 0), axis=0)  14 us
    all_to_all x1, waiting for transfers between devices, local(): strip = jnp.sum(lax.all_to_all(copies(part, row_size), 'row', 0, 0), axis=0)  11.1 us
    all_to_all x1, waiting for transfers between devices, local(): lax.all_to_all(copies((own * SAMPLE_SCALE).astype(F16), col_size), 'col',...  8.04 us
    all_to_all x1, starting transfers between devices, local(): lax.all_to_all(copies(strip, col_size), 'col', 0, 0).reshape(width, width)  6.54 us
  transfers between devices with their start and end apart: 5, of which 5 were waited for; matrix products, arithmetic and copies ran while one was open for 5% of the time, Pallas kernels for 13%

profile of v1, /device:TPU:6, one launch (start us, length us, event | category | flops | bytes accessed | tf_op | source)
XLA Modules:
  0.0 166.5 jit_solution(9585488617150144389)
XLA Ops:
  0.6 0.0 copy-start
  0.6 1.9 %copy-done = bf16[768,2048]{1,0:T(8,128)(2,1)S(1)} copy-done((bf16[768,2048]{1,0:T(8,128)(2,1)S(1)}, bf16[768,2048]{1,0:T(8,128)(2,1)}, u32[]{:S(2)}) %copy-start) | copy-done | bytes 3145752
  2.5 2.2 %fusion = f16[768,256]{1,0:T(8,128)(2,1)S(1)} fusion(bf16[768,2048]{1,0:T(8,128)(2,1)S(1)} %copy-done, bf16[2048,256]{1,0:T(8,128)(2,1)} %param.3), kind=kOutput, calls=%fused_computation.3 | convolution fusion | flops 805699584 | bytes 4587520 | tf_op jit(solution)/shard_map/sample/dot_general | solution.py:96
  4.7 16.7 %all_to_all.30 = f16[32,24,256]{2,1,0:T(8,128)(2,1)S(1)} all-to-all(f16[32,24,256]{2,1,0:T(8,128)(2,1)S(1)} %bitcast.36), channel_id=1, replica_groups=mesh['row'=16,'col'=32] {'col'}, dimensions={0} | all-to-all | bytes 786432 | tf_op jit(solution)/shard_map/sample/all_to_all | solution.py:98
  21.4 0.1 convert_reduce_fusion
  21.5 0.0 copy-start.2
  21.5 0.6 copy-done.2
  22.1 0.8 broadcast_in_dim.6
  22.9 5.8 %all-to-all-start.1 = ((f16[32,24,256]{2,1,0:T(8,128)(2,1)}), f16[32,24,256]{2,1,0:T(8,128)(2,1)S(1)}, u32[]{:S(2)}, u32[]{:S(2)}) async-start(f16[32,24,256]{2,1,0:T(8,128)(2,1)} %broadcast_in_dim.6), calls=%async_computation.1 | async-start | bytes 786432 | tf_op jit(solution)/shard_map/sample/all_to_all | solution.py:100
  28.7 8.0 %all-to-all-done.1 = f16[32,24,256]{2,1,0:T(8,128)(2,1)S(1)} async-done(((f16[32,24,256]{2,1,0:T(8,128)(2,1)}), f16[32,24,256]{2,1,0:T(8,128)(2,1)S(1)}, u32[]{:S(2)}, u32[]{:S(2)}) %all-to-all-start.1) | async-done | bytes 393248 | tf_op jit(solution)/shard_map/sample/all_to_all | solution.py:100
  36.7 1.5 convolution_bitcast_fusion
  38.3 0.7 broadcast_in_dim.7
  38.9 14.0 %all-to-all-start.2 = ((f32[16,8,256]{2,1,0:T(8,128)}), f32[16,8,256]{2,1,0:T(8,128)}, u32[]{:S(2)}, u32[]{:S(2)}) async-start(f32[16,8,256]{2,1,0:T(8,128)} %broadcast_in_dim.7), calls=%async_computation.2 | async-start | bytes 262144 | tf_op jit(solution)/shard_map/gram/all_to_all | solution.py:105
  53.0 0.1 convert_multiply_fusion
  53.1 0.5 copy.13
  53.6 0.1 fusion.2
  53.6 2.3 %fusion.8 = f32[256,2048]{1,0:T(8,128)} fusion(bf16[768,256]{1,0:T(8,128)(2,1)S(1)} %get-tuple-element.3, bf16[768,2048]{1,0:T(8,128)(2,1)S(1)} %copy-done), kind=kOutput, calls=%fused_computation.21 | convolution fusion | flops 805306368 | bytes 5636096 | tf_op jit(solution)/shard_map/product/dot_general | solution.py:110
  56.0 11.1 %all-to-all-done.2 = f32[16,8,256]{2,1,0:T(8,128)} async-done(((f32[16,8,256]{2,1,0:T(8,128)}), f32[16,8,256]{2,1,0:T(8,128)}, u32[]{:S(2)}, u32[]{:S(2)}) %all-to-all-start.2) | async-done | bytes 131104 | tf_op jit(solution)/shard_map/gram/all_to_all | solution.py:105
  67.1 0.9 reduce_sum.37
  68.0 0.7 broadcast_in_dim.8
  68.7 6.5 %all-to-all-start.3 = ((f32[32,8,256]{2,1,0:T(8,128)}), f32[32,8,256]{2,1,0:T(8,128)}, u32[]{:S(2)}, u32[]{:S(2)}) async-start(f32[32,8,256]{2,1,0:T(8,128)} %broadcast_in_dim.8), calls=%async_computation.3 | async-start | bytes 524288 | tf_op jit(solution)/shard_map/gram/all_to_all | solution.py:106
  75.2 2.6 %convolution_add_fusion = f32[256,2048]{1,0:T(8,128)S(1)} fusion(f32[256,2048]{1,0:T(8,128)} %fusion.8, bf16[768,256]{1,0:T(8,128)(2,1)S(1)} %get-tuple-element.2, bf16[768,2048]{1,0:T(8,128)(2,1)S(1)} %copy-done), kind=kOutput, calls=%fused_computation | convolution fusion | flops 805830656 | bytes 7733248 | tf_op jit(solution)/shard_map/product/dot_general | solution.py:111
  77.8 1.5 copy.21
  79.4 2.9 %all-to-all-done.3 = f32[32,8,256]{2,1,0:T(8,128)} async-done(((f32[32,8,256]{2,1,0:T(8,128)}), f32[32,8,256]{2,1,0:T(8,128)}, u32[]{:S(2)}, u32[]{:S(2)}) %all-to-all-start.3) | async-done | bytes 262176 | tf_op jit(solution)/shard_map/gram/all_to_all | solution.py:106
  82.3 4.6 %all-to-all-start.4 = ((f32[4,256,512]{2,1,0:T(8,128)}), f32[4,256,512]{2,1,0:T(8,128)}, u32[]{:S(2)}, u32[]{:S(2)}) async-start(f32[4,256,512]{2,1,0:T(8,128)} %bitcast.33), calls=%async_computation.4 | async-start | bytes 4194304 | tf_op jit(solution)/shard_map/product/all_to_all | solution.py:113
  86.9 0.0 copy-start.3
  86.9 21.6 %inverse_factor.1 = f32[256,256]{1,0:T(8,128)} custom-call(f32[256,256]{1,0:T(8,128)} %bitcast.2.gram_ref), custom_call_target="tpu_custom_call" | custom-call | tf_op jit(solution)/shard_map/factor/inverse_factor/pallas_call | solution.py:75
  108.5 0.0 copy-start.1
  108.5 27.5 %all-to-all-done.4 = f32[4,256,512]{2,1,0:T(8,128)} async-done(((f32[4,256,512]{2,1,0:T(8,128)}), f32[4,256,512]{2,1,0:T(8,128)}, u32[]{:S(2)}, u32[]{:S(2)}) %all-to-all-start.4) | async-done | bytes 2097184 | tf_op jit(solution)/shard_map/product/all_to_all | solution.py:113
  136.0 2.7 %reduce_sum.38 = f32[256,512]{1,0:T(8,128)} reduce(f32[4,256,512]{2,1,0:T(8,128)} %all-to-all-done.4, f32[]{:T(128)} %constant.10.clone.1), dimensions={0}, to_apply=%region_2.0 | reduce | flops 393216 | bytes 2621444 | tf_op jit(solution)/shard_map/product/reduce_sum | solution.py:113
  138.7 2.4 %fusion.1 = f16[256,512]{1,0:T(8,128)(2,1)} fusion(f32[256,256]{1,0:T(8,128)} %inverse_factor.1, f32[256,512]{1,0:T(8,128)} %reduce_sum.38), kind=kOutput, calls=%fused_computation.5 | convolution fusion | flops 402915328 | bytes 1048576 | tf_op jit(solution)/shard_map/projected/dot_general | solution.py:119
  141.1 5.5 %all-to-all-start.5 = ((f16[16,16,512]{2,1,0:T(8,128)(2,1)}), f16[16,16,512]{2,1,0:T(8,128)(2,1)}, u32[]{:S(2)}, u32[]{:S(2)}) async-start(f16[16,16,512]{2,1,0:T(8,128)(2,1)} %bitcast.35), calls=%async_computation.5 | async-start | bytes 524288 | tf_op jit(solution)/shard_map/projected/all_to_all | solution.py:121
  146.6 0.0 copy-done.3
  146.6 0.0 copy-done.1
  146.6 0.9 fusion.3
  147.6 17.2 %all-to-all-done.5 = f16[16,16,512]{2,1,0:T(8,128)(2,1)} async-done(((f16[16,16,512]{2,1,0:T(8,128)(2,1)}), f16[16,16,512]{2,1,0:T(8,128)(2,1)}, u32[]{:S(2)}, u32[]{:S(2)}) %all-to-all-start.5) | async-done | bytes 262176 | tf_op jit(solution)/shard_map/projected/all_to_all | solution.py:121
  164.8 1.0 convert_reduce_fusion.1
  165.8 0.7 copy.17
  (3 shorter events, 0.0 us)
Async XLA Ops:
  0.6 1.9 %copy-start = (bf16[768,2048]{1,0:T(8,128)(2,1)S(1)}, bf16[768,2048]{1,0:T(8,128)(2,1)}, u32[]{:S(2)}) copy-start(bf16[768,2048]{1,0:T(8,128)(2,1)} %param.2) | copy-start | bytes 9437188
  21.5 0.6 copy-start.2
  22.9 13.8 %all-to-all-start.1 = ((f16[32,24,256]{2,1,0:T(8,128)(2,1)}), f16[32,24,256]{2,1,0:T(8,128)(2,1)S(1)}, u32[]{:S(2)}, u32[]{:S(2)}) async-start(f16[32,24,256]{2,1,0:T(8,128)(2,1)} %broadcast_in_dim.6), calls=%async_computation.1 | async-start | bytes 786432 | tf_op jit(solution)/shard_map/sample/all_to_all | solution.py:100
  38.9 28.1 %all-to-all-start.2 = ((f32[16,8,256]{2,1,0:T(8,128)}), f32[16,8,256]{2,1,0:T(8,128)}, u32[]{:S(2)}, u32[]{:S(2)}) async-start(f32[16,8,256]{2,1,0:T(8,128)} %broadcast_in_dim.7), calls=%async_computation.2 | async-start | bytes 262144 | tf_op jit(solution)/shard_map/gram/all_to_all | solution.py:105
  68.7 13.6 %all-to-all-start.3 = ((f32[32,8,256]{2,1,0:T(8,128)}), f32[32,8,256]{2,1,0:T(8,128)}, u32[]{:S(2)}, u32[]{:S(2)}) async-start(f32[32,8,256]{2,1,0:T(8,128)} %broadcast_in_dim.8), calls=%async_computation.3 | async-start | bytes 524288 | tf_op jit(solution)/shard_map/gram/all_to_all | solution.py:106
  82.3 53.7 %all-to-all-start.4 = ((f32[4,256,512]{2,1,0:T(8,128)}), f32[4,256,512]{2,1,0:T(8,128)}, u32[]{:S(2)}, u32[]{:S(2)}) async-start(f32[4,256,512]{2,1,0:T(8,128)} %bitcast.33), calls=%async_computation.4 | async-start | bytes 4194304 | tf_op jit(solution)/shard_map/product/all_to_all | solution.py:113
  86.9 59.7 %copy-start.3 = (f32[24,256]{1,0:T(8,128)S(1)}, f32[24,256]{1,0:T(8,128)}, u32[]{:S(2)}) copy-start(f32[24,256]{1,0:T(8,128)} %copy-done.2) | copy-start | bytes 73732
  108.5 38.1 %copy-start.1 = (f32[256,256]{1,0:T(8,128)S(1)}, f32[256,256]{1,0:T(8,128)}, u32[]{:S(2)}) copy-start(f32[256,256]{1,0:T(8,128)} %inverse_factor.1) | copy-start | bytes 786436
  141.1 23.7 %all-to-all-start.5 = ((f16[16,16,512]{2,1,0:T(8,128)(2,1)}), f16[16,16,512]{2,1,0:T(8,128)(2,1)}, u32[]{:S(2)}, u32[]{:S(2)}) async-start(f16[16,16,512]{2,1,0:T(8,128)(2,1)} %bitcast.35), calls=%async_computation.5 | async-start | bytes 524288 | tf_op jit(solution)/shard_map/projected/all_to_all | solution.py:121

commit v2 on v1

v2 whole, which is shorter than its diff:
```python
import jax
import jax.numpy as jnp
from jax import lax
from jax.experimental import pallas as pl
from jax.experimental.pallas import tpu as pltpu
from jax.sharding import PartitionSpec as P

F32 = jnp.float32
F16 = jnp.float16
BF16 = jnp.bfloat16
EXACT = lax.Precision.HIGHEST
TILE = 64
GROUP = 4
SKETCH_SCALE = 128.0
SAMPLE_SCALE = 4.0
PROJ_SCALE = 128.0


def eliminate(tile, out_ref, n):
    groups = [tile[8 * g : 8 * g + 8, :] for g in range(n // 8)]
    shape = groups[0].shape
    spread = lambda v: jnp.broadcast_to(v, shape)
    for g in range(n // 8):
        j = 8 * g
        later = range(g + 1, n // 8)
        own = [spread(groups[g][:, j + k : j + k + 1]) for k in range(8)]
        cols = {h: [spread(groups[h][:, j + k : j + k + 1]) for k in range(8)] for h in later}
        s = [[spread(own[k][i : i + 1, :]) for k in range(i + 1)] for i in range(8)]
        rows = [spread(groups[g][i : i + 1, :]) for i in range(8)]
        for k in range(0, 8, 2):
            a, b, c = s[k][k], s[k + 1][k], s[k + 1][k + 1]
            det = a * c - b * b
            inv = 1.0 / det
            pa, pb, pc = a * inv, b * inv, c * inv
            for i in range(k + 2, 8):
                m0 = pc * s[i][k] - pb * s[i][k + 1]
                m1 = pa * s[i][k + 1] - pb * s[i][k]
                for m in range(k + 2, i + 1):
                    s[i][m] = s[i][m] - (m0 * s[m][k] + m1 * s[m][k + 1])
                rows[i] = rows[i] - (m0 * rows[k] + m1 * rows[k + 1])
            for h in later:
                m0 = pc * cols[h][k] - pb * cols[h][k + 1]
                m1 = pa * cols[h][k + 1] - pb * cols[h][k]
                for m in range(k + 2, 8):
                    cols[h][m] = cols[h][m] - (m0 * s[m][k] + m1 * s[m][k + 1])
                groups[h] = groups[h] - (m0 * rows[k] + m1 * rows[k + 1])
            inv_a = 1.0 / a
            x0 = rows[k] * lax.rsqrt(a)
            x1 = (rows[k + 1] - (b * inv_a) * rows[k]) * lax.rsqrt(det * inv_a)
            out_ref[j + k : j + k + 1, :] = x0[0:1, :]
            out_ref[j + k + 1 : j + k + 2, :] = x1[0:1, :]


def eye(size):
    rows = lax.broadcasted_iota(jnp.int32, (size, size), 0)
    return (rows == lax.broadcasted_iota(jnp.int32, (size, size), 1)).astype(F32)


def factor_kernel(gram_ref, own_ref, mine_ref, left_ref, right_ref, up_ref, down_ref, basis_ref, proj_ref, aug, x_ref, inv):
    n = gram_ref.shape[0]
    half = n // 2
    aug[:, :n] = gram_ref[...]
    aug[:, n:] = eye(n)
    for k in range(n // TILE):
        lo, hi = k * TILE, (k + 1) * TILE
        tile = jnp.concatenate([aug[lo:hi, lo:hi], eye(TILE)], axis=1)
        eliminate(tile, x_ref, TILE)
        row = jnp.dot(x_ref[:, TILE:], aug[lo:hi, :], precision=EXACT, preferred_element_type=F32)
        inv[lo:hi, :] = row[:, n:]
        if hi < n:
            aug[hi:, :] = aug[hi:, :] - lax.dot_general(
                row[:, hi:n], row, (((0,), (0,)), ((), ())), precision=EXACT, preferred_element_type=F32
            )
    total = mine_ref[...] + left_ref[...] + right_ref[...]
    total = total + jnp.concatenate([up_ref[...], down_ref[...]], axis=0)
    proj_ref[...] = jnp.dot(inv[...], total, precision=EXACT, preferred_element_type=F32) * PROJ_SCALE
    basis_ref[...] = lax.dot_general(
        own_ref[...], inv[...], (((1,), (1,)), ((), ())), precision=EXACT, preferred_element_type=F32
    )


def factor_and_apply(gram, own, parts):
    n = gram.shape[0]
    return pl.pallas_call(
        factor_kernel,
        out_shape=(jax.ShapeDtypeStruct(own.shape, F32), jax.ShapeDtypeStruct(parts[0].shape, F32)),
        scratch_shapes=[pltpu.VMEM((n, 2 * n), F32), pltpu.VMEM((TILE, 2 * TILE), F32), pltpu.VMEM((n, n), F32)],
        compiler_params=pltpu.CompilerParams(vmem_limit_bytes=32 * 2**20),
        cost_estimate=pl.CostEstimate(flops=2 * 10**9, bytes_accessed=4 * 2**20, transcendentals=0),
        name="factor_and_apply",
    )(gram, own, *parts)


def product_kernel(sampled_ref, slab_ref, mine_ref, right_ref, left_ref, far_up_ref, far_down_ref):
    width = mine_ref.shape[1]
    half = mine_ref.shape[0] // 2
    at = lax.axis_index("row")
    sampled = sampled_ref[...]
    high = sampled.astype(BF16)
    low = (sampled - high.astype(F32)).astype(BF16)
    terms = jnp.concatenate([high, low], axis=1)

    def quarter(step):
        start = pl.multiple_of(lax.rem(at + step, GROUP) * width, width)
        both = lax.dot_general(
            terms, slab_ref[:, pl.ds(start, width)], (((0,), (0,)), ((), ())), preferred_element_type=F32
        )
        return both[: 2 * half] + both[2 * half :]

    mine_ref[...] = quarter(0)
    right_ref[...] = quarter(1)
    left_ref[...] = quarter(GROUP - 1)
    far = quarter(2)
    far_up_ref[...] = far[:half]
    far_down_ref[...] = far[half:]


def product_quarters(sampled, slab):
    n, width = sampled.shape[1], slab.shape[1] // GROUP
    whole = jax.ShapeDtypeStruct((n, width), F32)
    part = jax.ShapeDtypeStruct((n // 2, width), F32)
    return pl.pallas_call(
        product_kernel,
        out_shape=(whole, whole, whole, part, part),
        compiler_params=pltpu.CompilerParams(vmem_limit_bytes=32 * 2**20),
        cost_estimate=pl.CostEstimate(flops=16 * 10**8, bytes_accessed=6 * 2**20, transcendentals=0),
        name="product_quarters",
    )(sampled, slab)


def shift(x, step):
    size = lax.axis_size("row")
    return lax.ppermute(x, "row", [(i, (i + step) % size) for i in range(size)])


def copies(x, count):
    return jnp.broadcast_to(x[None], (count, *x.shape))


def local(slab, sketch):
    rows, cols = slab.shape
    width = sketch.shape[1]
    col_size, row_size = lax.axis_size("col"), lax.axis_size("row")
    share = rows // col_size
    piece = width // col_size
    out_rows = width // row_size
    with jax.named_scope("sample"):
        partial = jnp.dot(slab, sketch, preferred_element_type=F32)
        sent = (partial * SKETCH_SCALE).astype(F16).reshape(col_size, share, width)
        got = lax.all_to_all(sent, "col", 0, 0)
        own = jnp.sum(got.astype(F32), axis=0) * (1.0 / SKETCH_SCALE)
        shares = lax.all_to_all(copies((own * SAMPLE_SCALE).astype(F16), col_size), "col", 0, 0)
        sampled = shares.reshape(rows, width).astype(F32) * (1.0 / SAMPLE_SCALE)
    with jax.named_scope("gram"):
        part = lax.dot_general(sampled, sampled, (((0,), (0,)), ((), ())), precision=EXACT, preferred_element_type=F32)
        part = lax.dynamic_slice_in_dim(part, lax.axis_index("col") * piece, piece, 0)
        strip = jnp.sum(lax.all_to_all(copies(part, row_size), "row", 0, 0), axis=0)
        gram = lax.all_to_all(copies(strip, col_size), "col", 0, 0).reshape(width, width)
    with jax.named_scope("product"):
        mine, right, left, far_up, far_down = product_quarters(sampled, slab)
        parts = (mine, shift(right, 1), shift(left, -1), shift(far_up, 2), shift(far_down, -2))
    with jax.named_scope("factor"):
        basis, sent = factor_and_apply(gram, own, parts)
    with jax.named_scope("projected"):
        sent = sent.astype(F16).reshape(row_size, out_rows, cols // GROUP)
        got = lax.all_to_all(sent, "row", 0, 0).reshape(row_size // GROUP, GROUP, out_rows, cols // GROUP)
        projected = jnp.sum(got.astype(F32), axis=0) * (1.0 / PROJ_SCALE)
        projected = projected.transpose(1, 0, 2).reshape(out_rows, cols)
    return (basis, projected)


def solution(mesh):
    return jax.shard_map(
        local,
        mesh=mesh,
        in_specs=(P("row", "col"), P("col", None)),
        out_specs=(P(("row", "col"), None), P("row", "col")),
        check_vma=False,
    )
```

time: 169 us -> 135 us (0.80)
  waiting for transfers between devices: 66.8 us -> 18.1 us
  blocking collectives: 16.7 us -> 44.9 us
  matrix products: 12 us -> 4.36 us
  Pallas kernels: 21.6 us -> 14.9 us
  other arithmetic: 4.86 us -> 0.31 us
  starting transfers between devices: 36.5 us -> 40.6 us
    all_to_all x2 -> x0, waiting for transfers between devices: 44.8 us -> none  [the longest x1 27.5 us: local(): lax.all_to_all(product, 'row', 0, 0, axis_index_groups=neighbours)]
    all_to_all x0 -> x1, blocking collectives: none -> 28.2 us  [local(): lax.all_to_all(sent, 'row', 0, 0)]
    ppermute x0 -> x4, starting transfers between devices: none -> 15 us  [shift(): return lax.ppermute(x, 'row', [(i, (i + step) % size) for i in range(size)])]
    all_to_all x1, waiting for transfers between devices: 11.1 us -> 0.01 us  [local(): strip = jnp.sum(lax.all_to_all(copies(part, row_size), 'row', 0, 0), axis=0)]
    all_to_all x2 -> x0, starting transfers between devices: 10.1 us -> none  [the longest x1 5.47 us: local(): lax.all_to_all(sent, 'row', 0, 0)]
    ppermute x0 -> x4, waiting for transfers between devices: none -> 10 us  [shift(): return lax.ppermute(x, 'row', [(i, (i + step) % size) for i in range(size)])]
    dot_general x4 -> x0, matrix products: 8.3 us -> none  [the longest x1 2.59 us: local(): lax.dot_general(low, slab, (((0,), (0,)), ((), ())), preferred_element_ty...]
    pallas_call x1 -> x2, Pallas kernels: 21.6 us -> 14.9 us  [the longest x1 12.2 us: factor_and_apply(): pl.pallas_call(factor_kernel, out_shape=(jax.ShapeDtypeStruct(own.shape,...]
  transfers between devices with their start and end apart: 5 -> 7, of which waited for: 5 -> 3; matrix products, arithmetic and copies ran while one was open for 5% -> 1% of each run, Pallas kernels for 13% -> 2%
where the time goes in v2:
time: 135 us; the launch traced here: 132 us
  blocking collectives  44.9 us (33%)
  starting transfers between devices  40.6 us (30%)
  waiting for transfers between devices  18.1 us (13%)
  Pallas kernels  14.9 us (11%)
  local copies, waits for them, and re-layouts  8.23 us (6%)
  matrix products  4.36 us (3%)
    all_to_all x1, blocking collectives, local(): lax.all_to_all(sent, 'row', 0, 0)  28.2 us
    all_to_all x1, blocking collectives, local(): got = lax.all_to_all(sent, 'col', 0, 0)  16.7 us
    ppermute x4, starting transfers between devices, shift(): return lax.ppermute(x, 'row', [(i, (i + step) % size) for i in range(size)])  15 us
    all_to_all x1, starting transfers between devices, local(): strip = jnp.sum(lax.all_to_all(copies(part, row_size), 'row', 0, 0), axis=0)  14 us
    pallas_call x1, Pallas kernels, factor_and_apply(): pl.pallas_call(factor_kernel, out_shape=(jax.ShapeDtypeStruct(own.shape,...  12.2 us
    ppermute x4, waiting for transfers between devices, shift(): return lax.ppermute(x, 'row', [(i, (i + step) % size) for i in range(size)])  10 us
    all_to_all x1, waiting for transfers between devices, local(): lax.all_to_all(copies((own * SAMPLE_SCALE).astype(F16), col_size), 'col',...  8.04 us
    all_to_all x1, starting transfers between devices, local(): lax.all_to_all(copies(strip, col_size), 'col', 0, 0).reshape(width, width)  5.79 us
  transfers between devices with their start and end apart: 7, of which 3 were waited for; matrix products, arithmetic and copies ran while one was open for 1% of the time, Pallas kernels for 2%

profile of v2, /device:TPU:6, one launch (start us, length us, event | category | flops | bytes accessed | tf_op | source)
XLA Modules:
  0.0 132.1 jit_solution(13325368949110549965)
XLA Ops:
  0.6 0.0 copy-start
  0.6 1.2 copy-done
  1.9 2.9 %fusion = f16[768,256]{1,0:T(8,128)(2,1)S(1)} fusion(bf16[768,2048]{1,0:T(8,128)(2,1)} %slab_ref.1, bf16[2048,256]{1,0:T(8,128)(2,1)S(1)} %copy-done), kind=kOutput, calls=%fused_computation.1 | convolution fusion | flops 805699584 | bytes 4587520 | tf_op jit(solution)/shard_map/sample/dot_general | solution.py:148
  4.7 16.7 %all_to_all.25 = f16[32,24,256]{2,1,0:T(8,128)(2,1)S(1)} all-to-all(f16[32,24,256]{2,1,0:T(8,128)(2,1)S(1)} %bitcast.18), channel_id=1, replica_groups=mesh['row'=16,'col'=32] {'col'}, dimensions={0} | all-to-all | bytes 786432 | tf_op jit(solution)/shard_map/sample/all_to_all | solution.py:150
  21.4 0.1 convert_reduce_fusion
  21.5 0.8 broadcast_in_dim.6
  22.3 5.8 %all-to-all-start.1 = ((f16[32,24,256]{2,1,0:T(8,128)(2,1)}), f16[32,24,256]{2,1,0:T(8,128)(2,1)S(1)}, u32[]{:S(2)}, u32[]{:S(2)}) async-start(f16[32,24,256]{2,1,0:T(8,128)(2,1)} %broadcast_in_dim.6), calls=%async_computation.1 | async-start | bytes 786432 | tf_op jit(solution)/shard_map/sample/all_to_all | solution.py:152
  28.1 8.0 %all-to-all-done.1 = f16[32,24,256]{2,1,0:T(8,128)(2,1)S(1)} async-done(((f16[32,24,256]{2,1,0:T(8,128)(2,1)}), f16[32,24,256]{2,1,0:T(8,128)(2,1)S(1)}, u32[]{:S(2)}, u32[]{:S(2)}) %all-to-all-start.1) | async-done | bytes 393248 | tf_op jit(solution)/shard_map/sample/all_to_all | solution.py:152
  36.1 1.5 %convolution_bitcast_fusion = f32[256,256]{1,0:T(8,128)S(1)} fusion(f16[32,24,256]{2,1,0:T(8,128)(2,1)S(1)} %all-to-all-done.1), kind=kOutput, calls=%fused_computation.2 | convolution fusion | flops 604372992 | bytes 655360 | tf_op jit(solution)/shard_map/gram/dot_general | solution.py:155
  37.6 0.7 broadcast_in_dim.7
  38.3 14.0 %all-to-all-start.2 = ((f32[16,8,256]{2,1,0:T(8,128)}), f32[16,8,256]{2,1,0:T(8,128)S(1)}, u32[]{:S(2)}, u32[]{:S(2)}) async-start(f32[16,8,256]{2,1,0:T(8,128)} %broadcast_in_dim.7), calls=%async_computation.2 | async-start | bytes 262144 | tf_op jit(solution)/shard_map/gram/all_to_all | solution.py:157
  52.3 0.1 convert_multiply_fusion
  52.4 0.5 copy.11
  52.9 0.0 copy-start.1
  52.9 1.9 %copy-done.1 = bf16[768,2048]{1,0:T(8,128)(2,1)S(1)} copy-done((bf16[768,2048]{1,0:T(8,128)(2,1)S(1)}, bf16[768,2048]{1,0:T(8,128)(2,1)}, u32[]{:S(2)}) %copy-start.1) | copy-done | bytes 3145752
  54.8 2.6 %product_quarters.1 = (f32[256,512]{1,0:T(8,128)S(1)}, f32[256,512]{1,0:T(8,128)S(1)}, f32[256,512]{1,0:T(8,128)S(1)}, f32[128,512]{1,0:T(8,128)}, f32[128,512]{1,0:T(8,128)}) custom-call(f32[768,256]{1,0:T(8,128)S(1)} %bitcast.14, bf16[768,2048]{1,0:T(8,128)(2,1)S(1)} %copy-done.1), custom_call_target="tpu_custom_call" | custom-call | flops 1600000000 | bytes 6291456 | tf_op jit(solution)/shard_map/product/product_quarters/pallas_call | solution.py:122
  57.4 0.0 copy-start.2
  57.4 0.8 copy-done.2
  58.2 3.8 %collective-permute-start = (f32[256,512]{1,0:T(8,128)S(1)}, f32[256,512]{1,0:T(8,128)S(1)}, u32[]{:S(2)}, u32[]{:S(2)}) collective-permute-start(f32[256,512]{1,0:T(8,128)S(1)} %get-tuple-element.10), channel_id=1, source_target_pairs={{0,32},{32,64},{64,96},{96,128},{128,160},{160,192},{192,224},{224... | collective-permute-start | bytes 1572872 | tf_op jit(solution)/shard_map/product/ppermute | solution.py:133
  62.0 3.2 %collective-permute-start.1 = (f32[256,512]{1,0:T(8,128)S(1)}, f32[256,512]{1,0:T(8,128)S(1)}, u32[]{:S(2)}, u32[]{:S(2)}) collective-permute-start(f32[256,512]{1,0:T(8,128)S(1)} %get-tuple-element.11), channel_id=1, source_target_pairs={{0,480},{32,0},{64,32},{96,64},{128,96},{160,128},{192,160},{224,1... | collective-permute-start | bytes 1572872 | tf_op jit(solution)/shard_map/product/ppermute | solution.py:133
  65.3 3.5 %collective-permute-start.2 = (f32[128,512]{1,0:T(8,128)}, f32[128,512]{1,0:T(8,128)}, u32[]{:S(2)}, u32[]{:S(2)}) collective-permute-start(f32[128,512]{1,0:T(8,128)} %get-tuple-element.12), channel_id=1, source_target_pairs={{0,64},{32,96},{64,128},{96,160},{128,192},{160,224},{192,256},{22... | collective-permute-start | bytes 786440 | tf_op jit(solution)/shard_map/product/ppermute | solution.py:133
  68.8 4.4 %collective-permute-start.3 = (f32[128,512]{1,0:T(8,128)}, f32[128,512]{1,0:T(8,128)}, u32[]{:S(2)}, u32[]{:S(2)}) collective-permute-start(f32[128,512]{1,0:T(8,128)} %get-tuple-element.13), channel_id=1, source_target_pairs={{0,448},{32,480},{64,0},{96,32},{128,64},{160,96},{192,128},{224,1... | collective-permute-start | bytes 786440 | tf_op jit(solution)/shard_map/product/ppermute | solution.py:133
  73.2 0.0 all-to-all-done.2
  73.3 0.7 broadcast_in_dim.8
  74.0 5.8 %all-to-all-start.3 = ((f32[32,8,256]{2,1,0:T(8,128)}), f32[32,8,256]{2,1,0:T(8,128)S(1)}, u32[]{:S(2)}, u32[]{:S(2)}) async-start(f32[32,8,256]{2,1,0:T(8,128)} %broadcast_in_dim.8), calls=%async_computation.3 | async-start | bytes 524288 | tf_op jit(solution)/shard_map/gram/all_to_all | solution.py:158
  79.8 5.5 %collective-permute-done.2.up_ref = f32[128,512]{1,0:T(8,128)} collective-permute-done((f32[128,512]{1,0:T(8,128)}, f32[128,512]{1,0:T(8,128)}, u32[]{:S(2)}, u32[]{:S(2)}) %collective-permute-start.2) | collective-permute-done | bytes 262176 | tf_op jit(solution)/shard_map/product/ppermute | solution.py:133
  85.3 4.5 %collective-permute-done.3.down_ref = f32[128,512]{1,0:T(8,128)} collective-permute-done((f32[128,512]{1,0:T(8,128)}, f32[128,512]{1,0:T(8,128)}, u32[]{:S(2)}, u32[]{:S(2)}) %collective-permute-start.3) | collective-permute-done | bytes 262176 | tf_op jit(solution)/shard_map/product/ppermute | solution.py:133
  89.8 0.0 collective-permute-done.left_ref
  89.8 0.0 collective-permute-done.1.right_ref
  89.8 0.0 all-to-all-done.3
  89.8 0.0 copy-start.3
  89.8 1.0 copy-done.3
  90.8 12.2 %factor_and_apply.1 = (f32[24,256]{1,0:T(8,128)}, f32[256,512]{1,0:T(8,128)S(1)}) custom-call(f32[256,256]{1,0:T(8,128)S(1)} %bitcast.15, f32[24,256]{1,0:T(8,128)S(1)} %get-tuple-element.16.own_ref, f32[256,512]{1,0:T(8,128)S(1)} %copy-done.3, f32[256,512]{1,0:T(8,128)S(1)} %collective-permute-done.left_ref, ...), custom_call_target="tpu_custom_call" | custom-call | flops 2000000000 | bytes 4194304 | tf_op jit(solution)/shard_map/factor/factor_and_apply/pallas_call | solution.py:84
  103.1 28.2 %all_to_all.26 = f16[16,16,512]{2,1,0:T(8,128)(2,1)S(1)} all-to-all(f16[16,16,512]{2,1,0:T(8,128)(2,1)S(1)} %bitcast.16), channel_id=1, replica_groups=mesh['row'=16,'col'=32] {'row'}, dimensions={0} | all-to-all | bytes 524288 | tf_op jit(solution)/shard_map/projected/all_to_all | solution.py:166
  131.4 0.7 copy.13
  (6 shorter events, 0.1 us)
Async XLA Ops:
  0.6 1.2 copy-start
  22.3 13.8 %all-to-all-start.1 = ((f16[32,24,256]{2,1,0:T(8,128)(2,1)}), f16[32,24,256]{2,1,0:T(8,128)(2,1)S(1)}, u32[]{:S(2)}, u32[]{:S(2)}) async-start(f16[32,24,256]{2,1,0:T(8,128)(2,1)} %broadcast_in_dim.6), calls=%async_computation.1 | async-start | bytes 786432 | tf_op jit(solution)/shard_map/sample/all_to_all | solution.py:152
  38.3 34.9 %all-to-all-start.2 = ((f32[16,8,256]{2,1,0:T(8,128)}), f32[16,8,256]{2,1,0:T(8,128)S(1)}, u32[]{:S(2)}, u32[]{:S(2)}) async-start(f32[16,8,256]{2,1,0:T(8,128)} %broadcast_in_dim.7), calls=%async_computation.2 | async-start | bytes 262144 | tf_op jit(solution)/shard_map/gram/all_to_all | solution.py:157
  52.9 1.9 %copy-start.1 = (bf16[768,2048]{1,0:T(8,128)(2,1)S(1)}, bf16[768,2048]{1,0:T(8,128)(2,1)}, u32[]{:S(2)}) copy-start(bf16[768,2048]{1,0:T(8,128)(2,1)} %slab_ref.1) | copy-start | bytes 9437188
  57.4 0.8 copy-start.2
  58.2 31.6 %collective-permute-start = (f32[256,512]{1,0:T(8,128)S(1)}, f32[256,512]{1,0:T(8,128)S(1)}, u32[]{:S(2)}, u32[]{:S(2)}) collective-permute-start(f32[256,512]{1,0:T(8,128)S(1)} %get-tuple-element.10), channel_id=1, source_target_pairs={{0,32},{32,64},{64,96},{96,128},{128,160},{160,192},{192,224},{224... | collective-permute-start | bytes 1572872 | tf_op jit(solution)/shard_map/product/ppermute | solution.py:133
  62.0 27.8 %collective-permute-start.1 = (f32[256,512]{1,0:T(8,128)S(1)}, f32[256,512]{1,0:T(8,128)S(1)}, u32[]{:S(2)}, u32[]{:S(2)}) collective-permute-start(f32[256,512]{1,0:T(8,128)S(1)} %get-tuple-element.11), channel_id=1, source_target_pairs={{0,480},{32,0},{64,32},{96,64},{128,96},{160,128},{192,160},{224,1... | collective-permute-start | bytes 1572872 | tf_op jit(solution)/shard_map/product/ppermute | solution.py:133
  65.3 20.0 %collective-permute-start.2 = (f32[128,512]{1,0:T(8,128)}, f32[128,512]{1,0:T(8,128)}, u32[]{:S(2)}, u32[]{:S(2)}) collective-permute-start(f32[128,512]{1,0:T(8,128)} %get-tuple-element.12), channel_id=1, source_target_pairs={{0,64},{32,96},{64,128},{96,160},{128,192},{160,224},{192,256},{22... | collective-permute-start | bytes 786440 | tf_op jit(solution)/shard_map/product/ppermute | solution.py:133
  68.8 21.0 %collective-permute-start.3 = (f32[128,512]{1,0:T(8,128)}, f32[128,512]{1,0:T(8,128)}, u32[]{:S(2)}, u32[]{:S(2)}) collective-permute-start(f32[128,512]{1,0:T(8,128)} %get-tuple-element.13), channel_id=1, source_target_pairs={{0,448},{32,480},{64,0},{96,32},{128,64},{160,96},{192,128},{224,1... | collective-permute-start | bytes 786440 | tf_op jit(solution)/shard_map/product/ppermute | solution.py:133
  74.0 15.8 %all-to-all-start.3 = ((f32[32,8,256]{2,1,0:T(8,128)}), f32[32,8,256]{2,1,0:T(8,128)S(1)}, u32[]{:S(2)}, u32[]{:S(2)}) async-start(f32[32,8,256]{2,1,0:T(8,128)} %broadcast_in_dim.8), calls=%async_computation.3 | async-start | bytes 524288 | tf_op jit(solution)/shard_map/gram/all_to_all | solution.py:158
  89.8 1.0 copy-start.3

commit v3 on v2

--- a/solution.py
+++ b/solution.py
@@ -56,9 +56,8 @@
     return (rows == lax.broadcasted_iota(jnp.int32, (size, size), 1)).astype(F32)
 
 
-def factor_kernel(gram_ref, own_ref, mine_ref, left_ref, right_ref, up_ref, down_ref, basis_ref, proj_ref, aug, x_ref, inv):
+def factor_kernel(gram_ref, inv_ref, aug, x_ref):
     n = gram_ref.shape[0]
-    half = n // 2
     aug[:, :n] = gram_ref[...]
     aug[:, n:] = eye(n)
     for k in range(n // TILE):
@@ -66,66 +65,98 @@
         tile = jnp.concatenate([aug[lo:hi, lo:hi], eye(TILE)], axis=1)
         eliminate(tile, x_ref, TILE)
         row = jnp.dot(x_ref[:, TILE:], aug[lo:hi, :], precision=EXACT, preferred_element_type=F32)
-        inv[lo:hi, :] = row[:, n:]
+        inv_ref[lo:hi, :] = row[:, n:]
         if hi < n:
             aug[hi:, :] = aug[hi:, :] - lax.dot_general(
                 row[:, hi:n], row, (((0,), (0,)), ((), ())), precision=EXACT, preferred_element_type=F32
             )
-    total = mine_ref[...] + left_ref[...] + right_ref[...]
-    total = total + jnp.concatenate([up_ref[...], down_ref[...]], axis=0)
-    proj_ref[...] = jnp.dot(inv[...], total, precision=EXACT, preferred_element_type=F32) * PROJ_SCALE
-    basis_ref[...] = lax.dot_general(
-        own_ref[...], inv[...], (((1,), (1,)), ((), ())), precision=EXACT, preferred_element_type=F32
-    )
-
-
-def factor_and_apply(gram, own, parts):
+
+
+def inverse_factor(gram):
     n = gram.shape[0]
     return pl.pallas_call(
         factor_kernel,
-        out_shape=(jax.ShapeDtypeStruct(own.shape, F32), jax.ShapeDtypeStruct(parts[0].shape, F32)),
-        scratch_shapes=[pltpu.VMEM((n, 2 * n), F32), pltpu.VMEM((TILE, 2 * TILE), F32), pltpu.VMEM((n, n), F32)],
-        compiler_params=pltpu.CompilerParams(vmem_limit_bytes=32 * 2**20),
-        cost_estimate=pl.CostEstimate(flops=2 * 10**9, bytes_accessed=4 * 2**20, transcendentals=0),
-        name="factor_and_apply",
-    )(gram, own, *parts)
-
-
-def product_kernel(sampled_ref, slab_ref, mine_ref, right_ref, left_ref, far_up_ref, far_down_ref):
-    width = mine_ref.shape[1]
-    half = mine_ref.shape[0] // 2
-    at = lax.axis_index("row")
-    sampled = sampled_ref[...]
-    high = sampled.astype(BF16)
-    low = (sampled - high.astype(F32)).astype(BF16)
-    terms = jnp.concatenate([high, low], axis=1)
-
-    def quarter(step):
-        start = pl.multiple_of(lax.rem(at + step, GROUP) * width, width)
-        both = lax.dot_general(
-            terms, slab_ref[:, pl.ds(start, width)], (((0,), (0,)), ((), ())), preferred_element_type=F32
-        )
-        return both[: 2 * half] + both[2 * half :]
-
-    mine_ref[...] = quarter(0)
-    right_ref[...] = quarter(1)
-    left_ref[...] = quarter(GROUP - 1)
-    far = quarter(2)
-    far_up_ref[...] = far[:half]
-    far_down_ref[...] = far[half:]
+        out_shape=jax.ShapeDtypeStruct((n, n), F32),
+        scratch_shapes=[pltpu.VMEM((n, 2 * n), F32), pltpu.VMEM((TILE, 2 * TILE), F32)],
+        compiler_params=pltpu.CompilerParams(vmem_limit_bytes=16 * 2**20),
+        cost_estimate=pl.CostEstimate(flops=10**8, bytes_accessed=2**20, transcendentals=0),
+        name="inverse_factor",
+    )(gram)
+
+
+def apply_kernel(inv_ref, mine_ref, left_ref, right_ref, up_ref, down_ref, proj_ref):
+    half = up_ref.shape[0]
+    near = mine_ref[...] + left_ref[...] + right_ref[...]
+    total = jnp.concatenate([near[:half] + up_ref[...], near[half:] + down_ref[...]], axis=0)
+    proj_ref[...] = jnp.dot(inv_ref[...], total, precision=EXACT, preferred_element_type=F32) * PROJ_SCALE
+
+
+def apply_inverse(inverse, parts):
+    return pl.pallas_call(
+        apply_kernel,
+        out_shape=jax.ShapeDtypeStruct(parts[0].shape, F32),
+        compiler_params=pltpu.CompilerParams(vmem_limit_bytes=16 * 2**20),
+        cost_estimate=pl.CostEstimate(flops=6 * 10**8, bytes_accessed=3 * 2**20, transcendentals=0),
+        name="apply_inverse",
+    )(inverse, *parts)
+
+
+def product_kernel(at_ref, sampled_ref, slab_ref, mine_ref, right_ref, left_ref, far_up_ref, far_down_ref, terms):
+    n, half = mine_ref.shape[0], far_up_ref.shape[0]
+    step = pl.program_id(0)
+
+    @pl.when(step == 0)
+    def _():
+        high = sampled_ref[...].astype(BF16)
+        terms[:, :n] = high
+        terms[:, n:] = (sampled_ref[...] - high.astype(F32)).astype(BF16)
+
+    both = lax.dot_general(terms[...], slab_ref[...], (((0,), (0,)), ((), ())), preferred_element_type=F32)
+    total = both[:n] + both[n:]
+
+    @pl.when(step == 0)
+    def _():
+        right_ref[...] = total
+
+    @pl.when(step == 1)
+    def _():
+        far_up_ref[...] = total[:half]
+        far_down_ref[...] = total[half:]
+
+    @pl.when(step == 2)
+    def _():
+        left_ref[...] = total
+
+    @pl.when(step == 3)
+    def _():
+        mine_ref[...] = total
 
 
 def product_quarters(sampled, slab):
-    n, width = sampled.shape[1], slab.shape[1] // GROUP
+    rows, n = sampled.shape
+    width = slab.shape[1] // GROUP
     whole = jax.ShapeDtypeStruct((n, width), F32)
     part = jax.ShapeDtypeStruct((n // 2, width), F32)
+    whole_spec = pl.BlockSpec((n, width), lambda step, at: (0, 0))
+    part_spec = pl.BlockSpec((n // 2, width), lambda step, at: (0, 0))
+    at = lax.axis_index("row").astype(jnp.int32).reshape(1)
     return pl.pallas_call(
         product_kernel,
         out_shape=(whole, whole, whole, part, part),
-        compiler_params=pltpu.CompilerParams(vmem_limit_bytes=32 * 2**20),
+        grid_spec=pltpu.PrefetchScalarGridSpec(
+            num_scalar_prefetch=1,
+            grid=(GROUP,),
+            in_specs=[
+                pl.BlockSpec((rows, n), lambda step, at: (0, 0)),
+                pl.BlockSpec((rows, width), lambda step, at: (0, lax.rem(at[0] + step + 1, GROUP))),
+            ],
+            out_specs=(whole_spec, whole_spec, whole_spec, part_spec, part_spec),
+            scratch_shapes=[pltpu.VMEM((rows, 2 * n), BF16)],
+        ),
+        compiler_params=pltpu.CompilerParams(vmem_limit_bytes=60 * 2**20),
         cost_estimate=pl.CostEstimate(flops=16 * 10**8, bytes_accessed=6 * 2**20, transcendentals=0),
         name="product_quarters",
-    )(sampled, slab)
+    )(at, sampled, slab)
 
 
 def shift(x, step):
@@ -155,14 +186,19 @@
         part = lax.dot_general(sampled, sampled, (((0,), (0,)), ((), ())), precision=EXACT, preferred_element_type=F32)
         part = lax.dynamic_slice_in_dim(part, lax.axis_index("col") * piece, piece, 0)
         strip = jnp.sum(lax.all_to_all(copies(part, row_size), "row", 0, 0), axis=0)
-        gram = lax.all_to_all(copies(strip, col_size), "col", 0, 0).reshape(width, width)
     with jax.named_scope("product"):
         mine, right, left, far_up, far_down = product_quarters(sampled, slab)
-        parts = (mine, shift(right, 1), shift(left, -1), shift(far_up, 2), shift(far_down, -2))
+        near = (mine, shift(right, 1), shift(left, -1))
+        far_up, far_down, strip = lax.optimization_barrier((far_up, far_down, strip))
+        parts = near + (shift(far_up, 2), shift(far_down, -2))
+    with jax.named_scope("gram"):
+        gram = lax.all_to_all(copies(strip, col_size), "col", 0, 0).reshape(width, width)
     with jax.named_scope("factor"):
-        basis, sent = factor_and_apply(gram, own, parts)
+        inverse = inverse_factor(gram)
+    with jax.named_scope("basis"):
+        basis = lax.dot_general(own, inverse, (((1,), (1,)), ((), ())), precision=EXACT, preferred_element_type=F32)
     with jax.named_scope("projected"):
-        sent = sent.astype(F16).reshape(row_size, out_rows, cols // GROUP)
+        sent = apply_inverse(inverse, parts).astype(F16).reshape(row_size, out_rows, cols // GROUP)
         got = lax.all_to_all(sent, "row", 0, 0).reshape(row_size // GROUP, GROUP, out_rows, cols // GROUP)
         projected = jnp.sum(got.astype(F32), axis=0) * (1.0 / PROJ_SCALE)
         projected = projected.transpose(1, 0, 2).reshape(out_rows, cols)

time: 135 us -> 126 us (0.933); the launches traced: 132 us -> 126 us
  blocking collectives: 44.9 us -> 16.7 us
  waiting for transfers between devices: 18.1 us -> 28.6 us
  starting transfers between devices: 40.6 us -> 50.2 us
  local copies, waits for them, and re-layouts: 8.23 us -> 6.47 us
  Pallas kernels: 14.9 us -> 16.6 us
    all_to_all x1 -> x0, blocking collectives: 28.2 us -> none  [local(): lax.all_to_all(sent, 'row', 0, 0)]
    all_to_all x0 -> x1, waiting for transfers between devices: none -> 16.9 us  [local(): lax.all_to_all(sent, 'row', 0, 0)]
    all_to_all x0 -> x1, starting transfers between devices: none -> 9.21 us  [local(): lax.all_to_all(sent, 'row', 0, 0)]
    ppermute x4, waiting for transfers between devices: 10 us -> 3.72 us  [shift(): return lax.ppermute(x, 'row', [(i, (i + step) % size) for i in range(size)])]
    pallas_call x1, Pallas kernels: 2.62 us -> 5.96 us  [product_quarters(): pl.pallas_call(product_kernel, out_shape=(whole, whole, whole, part, part...]
    unnamed x8 -> x4, local copies, waits for them, and re-layouts: 4.94 us -> 2.26 us
    pallas_call x1 -> x2, Pallas kernels: 12.2 us -> 10.6 us  [the longest x1 9.94 us: inverse_factor(): pl.pallas_call(factor_kernel, out_shape=jax.ShapeDtypeStruct((n, n), F32)...]
  transfers between devices with their start and end apart: 7 -> 8, of which waited for: 3 -> 4; matrix products, arithmetic and copies ran while one was open for 1% -> 3% of each run, Pallas kernels for 2% -> 13%
where the time goes in v3:
time: 126 us
  starting transfers between devices  50.2 us (40%)
  waiting for transfers between devices  28.6 us (23%)
  blocking collectives  16.7 us (13%)
  Pallas kernels  16.6 us (13%)
  local copies, waits for them, and re-layouts  6.47 us (5%)
  matrix products  5.3 us (4%)
    all_to_all x1, waiting for transfers between devices, local(): lax.all_to_all(sent, 'row', 0, 0)  16.9 us
    all_to_all x1, blocking collectives, local(): got = lax.all_to_all(sent, 'col', 0, 0)  16.7 us
    ppermute x4, starting transfers between devices, shift(): return lax.ppermute(x, 'row', [(i, (i + step) % size) for i in range(size)])  15.2 us
    all_to_all x1, starting transfers between devices, local(): strip = jnp.sum(lax.all_to_all(copies(part, row_size), 'row', 0, 0), axis=0)  14 us
    pallas_call x1, Pallas kernels, inverse_factor(): pl.pallas_call(factor_kernel, out_shape=jax.ShapeDtypeStruct((n, n), F32)...  9.94 us
    all_to_all x1, starting transfers between devices, local(): lax.all_to_all(sent, 'row', 0, 0)  9.21 us
    all_to_all x1, waiting for transfers between devices, local(): lax.all_to_all(copies((own * SAMPLE_SCALE).astype(F16), col_size), 'col',...  8.04 us
    all_to_all x1, starting transfers between devices, local(): lax.all_to_all(copies(strip, col_size), 'col', 0, 0).reshape(width, width)  6.01 us
  transfers between devices with their start and end apart: 8, of which 4 were waited for; matrix products, arithmetic and copies ran while one was open for 3% of the time, Pallas kernels for 13%

profile of v3, /device:TPU:6, one launch (start us, length us, event | category | flops | bytes accessed | tf_op | source)
XLA Modules:
  0.0 125.6 jit_solution(14929345135973942017)
XLA Ops:
  0.6 0.0 copy-start
  0.6 1.2 copy-done
  1.9 2.9 %fusion = f16[768,256]{1,0:T(8,128)(2,1)S(1)} fusion(bf16[768,2048]{1,0:T(8,128)(2,1)} %slab_ref.1, bf16[2048,256]{1,0:T(8,128)(2,1)S(1)} %copy-done), kind=kOutput, calls=%fused_computation.1 | convolution fusion | flops 805699584 | bytes 4587520 | tf_op jit(solution)/shard_map/sample/dot_general | solution.py:179
  4.7 16.7 %all_to_all.25 = f16[32,24,256]{2,1,0:T(8,128)(2,1)S(1)} all-to-all(f16[32,24,256]{2,1,0:T(8,128)(2,1)S(1)} %bitcast.19), channel_id=1, replica_groups=mesh['row'=16,'col'=32] {'col'}, dimensions={0} | all-to-all | bytes 786432 | tf_op jit(solution)/shard_map/sample/all_to_all | solution.py:181
  21.4 0.1 convert_reduce_fusion
  21.5 0.8 broadcast_in_dim.6
  22.3 5.8 %all-to-all-start.1 = ((f16[32,24,256]{2,1,0:T(8,128)(2,1)}), f16[32,24,256]{2,1,0:T(8,128)(2,1)S(1)}, u32[]{:S(2)}, u32[]{:S(2)}) async-start(f16[32,24,256]{2,1,0:T(8,128)(2,1)} %broadcast_in_dim.6), calls=%async_computation.1 | async-start | bytes 786432 | tf_op jit(solution)/shard_map/sample/all_to_all | solution.py:183
  28.1 8.0 %all-to-all-done.1 = f16[32,24,256]{2,1,0:T(8,128)(2,1)S(1)} async-done(((f16[32,24,256]{2,1,0:T(8,128)(2,1)}), f16[32,24,256]{2,1,0:T(8,128)(2,1)S(1)}, u32[]{:S(2)}, u32[]{:S(2)}) %all-to-all-start.1) | async-done | bytes 393248 | tf_op jit(solution)/shard_map/sample/all_to_all | solution.py:183
  36.1 1.5 %convolution_bitcast_fusion = f32[256,256]{1,0:T(8,128)S(1)} fusion(f16[32,24,256]{2,1,0:T(8,128)(2,1)S(1)} %all-to-all-done.1), kind=kOutput, calls=%fused_computation.2 | convolution fusion | flops 604372992 | bytes 655360 | tf_op jit(solution)/shard_map/gram/dot_general | solution.py:186
  37.7 0.7 broadcast_in_dim.7
  38.3 14.0 %all-to-all-start.2 = ((f32[16,8,256]{2,1,0:T(8,128)}), f32[16,8,256]{2,1,0:T(8,128)S(1)}, u32[]{:S(2)}, u32[]{:S(2)}) async-start(f32[16,8,256]{2,1,0:T(8,128)} %broadcast_in_dim.7), calls=%async_computation.2 | async-start | bytes 262144 | tf_op jit(solution)/shard_map/gram/all_to_all | solution.py:188
  52.3 0.1 convert_multiply_fusion
  52.4 1.4 %copy.11 = f32[32,24,256]{2,1,0:T(8,128)} copy(f32[32,24,256]{2,0,1:T(8,128)S(1)} %convert_multiply_fusion) | data formatting | bytes 1572864 | tf_op jit(solution)/shard_map/sample/mul | solution.py:184
  53.8 6.0 %product_quarters.1 = (f32[256,512]{1,0:T(8,128)}, f32[256,512]{1,0:T(8,128)}, f32[256,512]{1,0:T(8,128)}, f32[128,512]{1,0:T(8,128)}, f32[128,512]{1,0:T(8,128)}) custom-call(s32[1]{0:T(128)} %bitcast.1.at_ref, f32[768,256]{1,0:T(8,128)} %bitcast.18, bf16[768,2048]{1,0:T(8,128)(2,1)} %slab_ref.1), custom_call_target="tpu_custom_call" | custom-call | flops 1600000000 | bytes 6291456 | tf_op jit(solution)/shard_map/product/product_quarters/pallas_call | solution.py:143
  59.8 3.8 %collective-permute-start = (f32[256,512]{1,0:T(8,128)}, f32[256,512]{1,0:T(8,128)S(1)}, u32[]{:S(2)}, u32[]{:S(2)}) collective-permute-start(f32[256,512]{1,0:T(8,128)} %get-tuple-element.14), channel_id=1, source_target_pairs={{0,32},{32,64},{64,96},{96,128},{128,160},{160,192},{192,224},{224... | collective-permute-start | bytes 1572872 | tf_op jit(solution)/shard_map/product/ppermute | solution.py:164
  63.6 3.2 %collective-permute-start.1 = (f32[256,512]{1,0:T(8,128)}, f32[256,512]{1,0:T(8,128)S(1)}, u32[]{:S(2)}, u32[]{:S(2)}) collective-permute-start(f32[256,512]{1,0:T(8,128)} %get-tuple-element.15), channel_id=1, source_target_pairs={{0,480},{32,0},{64,32},{96,64},{128,96},{160,128},{192,160},{224,1... | collective-permute-start | bytes 1572872 | tf_op jit(solution)/shard_map/product/ppermute | solution.py:164
  66.8 0.0 all-to-all-done.2
  66.9 0.7 broadcast_in_dim.8
  67.6 6.0 %all-to-all-start.3 = ((f32[32,8,256]{2,1,0:T(8,128)}), f32[32,8,256]{2,1,0:T(8,128)S(1)}, u32[]{:S(2)}, u32[]{:S(2)}) async-start(f32[32,8,256]{2,1,0:T(8,128)} %broadcast_in_dim.8), calls=%async_computation.3 | async-start | bytes 524288 | tf_op jit(solution)/shard_map/gram/all_to_all | solution.py:195
  73.6 4.1 %collective-permute-start.2 = (f32[128,512]{1,0:T(8,128)}, f32[128,512]{1,0:T(8,128)S(1)}, u32[]{:S(2)}, u32[]{:S(2)}) collective-permute-start(f32[128,512]{1,0:T(8,128)} %get-tuple-element.16), channel_id=1, source_target_pairs={{0,64},{32,96},{64,128},{96,160},{128,192},{160,224},{192,256},{22... | collective-permute-start | bytes 786440 | tf_op jit(solution)/shard_map/product/ppermute | solution.py:164
  77.7 4.0 %collective-permute-start.3 = (f32[128,512]{1,0:T(8,128)}, f32[128,512]{1,0:T(8,128)S(1)}, u32[]{:S(2)}, u32[]{:S(2)}) collective-permute-start(f32[128,512]{1,0:T(8,128)} %get-tuple-element.17), channel_id=1, source_target_pairs={{0,448},{32,480},{64,0},{96,32},{128,64},{160,96},{192,128},{224,1... | collective-permute-start | bytes 786440 | tf_op jit(solution)/shard_map/product/ppermute | solution.py:164
  81.7 0.0 all-to-all-done.3
  81.8 9.9 %inverse_factor.1.inv_ref = f32[256,256]{1,0:T(8,128)S(1)} custom-call(f32[256,256]{1,0:T(8,128)S(1)} %bitcast.16), custom_call_target="tpu_custom_call" | custom-call | flops 100000000 | bytes 1048576 | tf_op jit(solution)/shard_map/factor/inverse_factor/pallas_call | solution.py:77
  91.7 0.0 collective-permute-done.left_ref
  91.7 0.0 collective-permute-done.1.right_ref
  91.7 0.1 collective-permute-done.2.up_ref
  91.8 3.6 %collective-permute-done.3.down_ref = f32[128,512]{1,0:T(8,128)S(1)} collective-permute-done((f32[128,512]{1,0:T(8,128)}, f32[128,512]{1,0:T(8,128)S(1)}, u32[]{:S(2)}, u32[]{:S(2)}) %collective-permute-start.3) | collective-permute-done | bytes 262176 | tf_op jit(solution)/shard_map/product/ppermute | solution.py:164
  95.4 0.0 copy-start.1
  95.4 1.0 copy-done.1
  96.5 0.7 apply_inverse.1
  97.2 0.7 convert_element_type.32
  97.9 9.2 %all-to-all-start.4 = ((f16[16,16,512]{2,1,0:T(8,128)(2,1)}), f16[16,16,512]{2,1,0:T(8,128)(2,1)S(1)}, u32[]{:S(2)}, u32[]{:S(2)}) async-start(f16[16,16,512]{2,1,0:T(8,128)(2,1)} %bitcast.5), calls=%async_computation.4 | async-start | bytes 524288 | tf_op jit(solution)/shard_map/projected/all_to_all | solution.py:202
  107.1 0.9 fusion.1
  108.1 16.9 %all-to-all-done.4 = f16[16,16,512]{2,1,0:T(8,128)(2,1)S(1)} async-done(((f16[16,16,512]{2,1,0:T(8,128)(2,1)}), f16[16,16,512]{2,1,0:T(8,128)(2,1)S(1)}, u32[]{:S(2)}, u32[]{:S(2)}) %all-to-all-start.4) | async-done | bytes 262176 | tf_op jit(solution)/shard_map/projected/all_to_all | solution.py:202
  125.0 0.7 copy.13
  (5 shorter events, 0.1 us)
Async XLA Ops:
  0.6 1.2 copy-start
  22.3 13.8 %all-to-all-start.1 = ((f16[32,24,256]{2,1,0:T(8,128)(2,1)}), f16[32,24,256]{2,1,0:T(8,128)(2,1)S(1)}, u32[]{:S(2)}, u32[]{:S(2)}) async-start(f16[32,24,256]{2,1,0:T(8,128)(2,1)} %broadcast_in_dim.6), calls=%async_computation.1 | async-start | bytes 786432 | tf_op jit(solution)/shard_map/sample/all_to_all | solution.py:183
  38.3 28.5 %all-to-all-start.2 = ((f32[16,8,256]{2,1,0:T(8,128)}), f32[16,8,256]{2,1,0:T(8,128)S(1)}, u32[]{:S(2)}, u32[]{:S(2)}) async-start(f32[16,8,256]{2,1,0:T(8,128)} %broadcast_in_dim.7), calls=%async_computation.2 | async-start | bytes 262144 | tf_op jit(solution)/shard_map/gram/all_to_all | solution.py:188
  59.8 31.9 %collective-permute-start = (f32[256,512]{1,0:T(8,128)}, f32[256,512]{1,0:T(8,128)S(1)}, u32[]{:S(2)}, u32[]{:S(2)}) collective-permute-start(f32[256,512]{1,0:T(8,128)} %get-tuple-element.14), channel_id=1, source_target_pairs={{0,32},{32,64},{64,96},{96,128},{128,160},{160,192},{192,224},{224... | collective-permute-start | bytes 1572872 | tf_op jit(solution)/shard_map/product/ppermute | solution.py:164
  63.6 28.1 %collective-permute-start.1 = (f32[256,512]{1,0:T(8,128)}, f32[256,512]{1,0:T(8,128)S(1)}, u32[]{:S(2)}, u32[]{:S(2)}) collective-permute-start(f32[256,512]{1,0:T(8,128)} %get-tuple-element.15), channel_id=1, source_target_pairs={{0,480},{32,0},{64,32},{96,64},{128,96},{160,128},{192,160},{224,1... | collective-permute-start | bytes 1572872 | tf_op jit(solution)/shard_map/product/ppermute | solution.py:164
  67.6 14.2 %all-to-all-start.3 = ((f32[32,8,256]{2,1,0:T(8,128)}), f32[32,8,256]{2,1,0:T(8,128)S(1)}, u32[]{:S(2)}, u32[]{:S(2)}) async-start(f32[32,8,256]{2,1,0:T(8,128)} %broadcast_in_dim.8), calls=%async_computation.3 | async-start | bytes 524288 | tf_op jit(solution)/shard_map/gram/all_to_all | solution.py:195
  73.6 18.2 %collective-permute-start.2 = (f32[128,512]{1,0:T(8,128)}, f32[128,512]{1,0:T(8,128)S(1)}, u32[]{:S(2)}, u32[]{:S(2)}) collective-permute-start(f32[128,512]{1,0:T(8,128)} %get-tuple-element.16), channel_id=1, source_target_pairs={{0,64},{32,96},{64,128},{96,160},{128,192},{160,224},{192,256},{22... | collective-permute-start | bytes 786440 | tf_op jit(solution)/shard_map/product/ppermute | solution.py:164
  77.7 17.7 %collective-permute-start.3 = (f32[128,512]{1,0:T(8,128)}, f32[128,512]{1,0:T(8,128)S(1)}, u32[]{:S(2)}, u32[]{:S(2)}) collective-permute-start(f32[128,512]{1,0:T(8,128)} %get-tuple-element.17), channel_id=1, source_target_pairs={{0,448},{32,480},{64,0},{96,32},{128,64},{160,96},{192,128},{224,1... | collective-permute-start | bytes 786440 | tf_op jit(solution)/shard_map/product/ppermute | solution.py:164
  95.4 1.0 copy-start.1
  97.9 27.0 %all-to-all-start.4 = ((f16[16,16,512]{2,1,0:T(8,128)(2,1)}), f16[16,16,512]{2,1,0:T(8,128)(2,1)S(1)}, u32[]{:S(2)}, u32[]{:S(2)}) async-start(f16[16,16,512]{2,1,0:T(8,128)(2,1)} %bitcast.5), calls=%async_computation.4 | async-start | bytes 524288 | tf_op jit(solution)/shard_map/projected/all_to_all | solution.py:202

commit v4 on v3

--- a/solution.py
+++ b/solution.py
@@ -10,6 +10,8 @@
 BF16 = jnp.bfloat16
 EXACT = lax.Precision.HIGHEST
 TILE = 64
+LANES = 128
+PRODUCT_MIB = 50
 GROUP = 4
 SKETCH_SCALE = 128.0
 SAMPLE_SCALE = 4.0
@@ -64,11 +66,14 @@
         lo, hi = k * TILE, (k + 1) * TILE
         tile = jnp.concatenate([aug[lo:hi, lo:hi], eye(TILE)], axis=1)
         eliminate(tile, x_ref, TILE)
-        row = jnp.dot(x_ref[:, TILE:], aug[lo:hi, :], precision=EXACT, preferred_element_type=F32)
-        inv_ref[lo:hi, :] = row[:, n:]
+        first, last = hi // LANES * LANES, n + pl.cdiv(hi, LANES) * LANES
+        row = jnp.dot(x_ref[:, TILE:], aug[lo:hi, first:last], precision=EXACT, preferred_element_type=F32)
+        inv_ref[lo:hi, : last - n] = row[:, n - first :]
+        if last < 2 * n:
+            inv_ref[lo:hi, last - n :] = jnp.zeros((TILE, 2 * n - last), F32)
         if hi < n:
-            aug[hi:, :] = aug[hi:, :] - lax.dot_general(
-                row[:, hi:n], row, (((0,), (0,)), ((), ())), precision=EXACT, preferred_element_type=F32
+            aug[hi:, first:last] = aug[hi:, first:last] - lax.dot_general(
+                row[:, hi - first : n - first], row, (((0,), (0,)), ((), ())), precision=EXACT, preferred_element_type=F32
             )
 
 
@@ -101,62 +106,47 @@
     )(inverse, *parts)
 
 
-def product_kernel(at_ref, sampled_ref, slab_ref, mine_ref, right_ref, left_ref, far_up_ref, far_down_ref, terms):
-    n, half = mine_ref.shape[0], far_up_ref.shape[0]
-    step = pl.program_id(0)
-
-    @pl.when(step == 0)
-    def _():
-        high = sampled_ref[...].astype(BF16)
-        terms[:, :n] = high
-        terms[:, n:] = (sampled_ref[...] - high.astype(F32)).astype(BF16)
-
-    both = lax.dot_general(terms[...], slab_ref[...], (((0,), (0,)), ((), ())), preferred_element_type=F32)
-    total = both[:n] + both[n:]
-
-    @pl.when(step == 0)
-    def _():
-        right_ref[...] = total
-
-    @pl.when(step == 1)
-    def _():
-        far_up_ref[...] = total[:half]
-        far_down_ref[...] = total[half:]
-
-    @pl.when(step == 2)
-    def _():
-        left_ref[...] = total
-
-    @pl.when(step == 3)
-    def _():
-        mine_ref[...] = total
+def product_kernel(sampled_ref, slab_ref, mine_ref, right_ref, left_ref, far_up_ref, far_down_ref, held, sems):
+    half, width = far_up_ref.shape
+    at = lax.axis_index("row")
+
+    def load(step):
+        start = pl.multiple_of(lax.rem(at + step, GROUP) * width, width)
+        return pltpu.make_async_copy(slab_ref.at[:, pl.ds(start, width)], held.at[step], sems.at[step])
+
+    order = (1, 3, 2, 0)
+    for step in order:
+        load(step).start()
+    sampled = sampled_ref[...].T
+    high = sampled.astype(BF16)
+    low = (sampled - high.astype(F32)).astype(BF16)
+
+    def quarter(step):
+        load(step).wait()
+        total = jnp.dot(high, held[step], preferred_element_type=F32)
+        return total + jnp.dot(low, held[step], preferred_element_type=F32)
+
+    right_ref[...] = quarter(1)
+    left_ref[...] = quarter(GROUP - 1)
+    far = quarter(2)
+    far_up_ref[...] = far[:half]
+    far_down_ref[...] = far[half:]
+    mine_ref[...] = quarter(0)
 
 
 def product_quarters(sampled, slab):
-    rows, n = sampled.shape
-    width = slab.shape[1] // GROUP
+    (rows, n), width = sampled.shape, slab.shape[1] // GROUP
     whole = jax.ShapeDtypeStruct((n, width), F32)
     part = jax.ShapeDtypeStruct((n // 2, width), F32)
-    whole_spec = pl.BlockSpec((n, width), lambda step, at: (0, 0))
-    part_spec = pl.BlockSpec((n // 2, width), lambda step, at: (0, 0))
-    at = lax.axis_index("row").astype(jnp.int32).reshape(1)
     return pl.pallas_call(
         product_kernel,
         out_shape=(whole, whole, whole, part, part),
-        grid_spec=pltpu.PrefetchScalarGridSpec(
-            num_scalar_prefetch=1,
-            grid=(GROUP,),
-            in_specs=[
-                pl.BlockSpec((rows, n), lambda step, at: (0, 0)),
-                pl.BlockSpec((rows, width), lambda step, at: (0, lax.rem(at[0] + step + 1, GROUP))),
-            ],
-            out_specs=(whole_spec, whole_spec, whole_spec, part_spec, part_spec),
-            scratch_shapes=[pltpu.VMEM((rows, 2 * n), BF16)],
-        ),
-        compiler_params=pltpu.CompilerParams(vmem_limit_bytes=60 * 2**20),
+        in_specs=[pl.BlockSpec(memory_space=pltpu.VMEM), pl.BlockSpec(memory_space=pl.ANY)],
+        scratch_shapes=[pltpu.VMEM((GROUP, rows, width), slab.dtype), pltpu.SemaphoreType.DMA((GROUP,))],
+        compiler_params=pltpu.CompilerParams(vmem_limit_bytes=PRODUCT_MIB * 2**20),
         cost_estimate=pl.CostEstimate(flops=16 * 10**8, bytes_accessed=6 * 2**20, transcendentals=0),
         name="product_quarters",
-    )(at, sampled, slab)
+    )(sampled, slab)
 
 
 def shift(x, step):

time: 126 us -> 124 us (0.984)
  local copies, waits for them, and re-layouts: 6.47 us -> 4.51 us
  waiting for transfers between devices: 28.6 us -> 30 us
    all_to_all x1, waiting for transfers between devices: 0.01 us -> 2.11 us  [local(): strip = jnp.sum(lax.all_to_all(copies(part, row_size), 'row', 0, 0), axis=0)]
    pallas_call x1, Pallas kernels: 5.96 us -> 4.26 us  [product_quarters(): pl.pallas_call(product_kernel, out_shape=(whole, whole, whole, part, part...]
    all_to_all x1, starting transfers between devices: 9.21 us -> 7.58 us  [local(): lax.all_to_all(sent, 'row', 0, 0)]
  transfers between devices with their start and end apart: 8 -> 8, of which waited for: 4 -> 4; matrix products, arithmetic and copies ran while one was open for 3% -> 2% of each run, Pallas kernels for 13% -> 11%
where the time goes in v4:
time: 124 us; the launch traced here: 123 us
  starting transfers between devices  49 us (40%)
  waiting for transfers between devices  30 us (24%)
  blocking collectives  16.7 us (13%)
  Pallas kernels  15.7 us (13%)
  matrix products  5.3 us (4%)
  local copies, waits for them, and re-layouts  4.51 us (4%)
    all_to_all x1, waiting for transfers between devices, local(): lax.all_to_all(sent, 'row', 0, 0)  16.8 us
    all_to_all x1, blocking collectives, local(): got = lax.all_to_all(sent, 'col', 0, 0)  16.7 us
    ppermute x4, starting transfers between devices, shift(): return lax.ppermute(x, 'row', [(i, (i + step) % size) for i in range(size)])  15.2 us
    all_to_all x1, starting transfers between devices, local(): strip = jnp.sum(lax.all_to_all(copies(part, row_size), 'row', 0, 0), axis=0)  14 us
    pallas_call x1, Pallas kernels, inverse_factor(): pl.pallas_call(factor_kernel, out_shape=jax.ShapeDtypeStruct((n, n), F32)...  9.8 us
    all_to_all x1, waiting for transfers between devices, local(): lax.all_to_all(copies((own * SAMPLE_SCALE).astype(F16), col_size), 'col',...  8.04 us
    all_to_all x1, starting transfers between devices, local(): lax.all_to_all(sent, 'row', 0, 0)  7.58 us
    all_to_all x1, starting transfers between devices, local(): lax.all_to_all(copies(strip, col_size), 'col', 0, 0).reshape(width, width)  6.49 us
  transfers between devices with their start and end apart: 8, of which 4 were waited for; matrix products, arithmetic and copies ran while one was open for 2% of the time, Pallas kernels for 11%

profile of v4, /device:TPU:6, one launch (start us, length us, event | category | flops | bytes accessed | tf_op | source)
XLA Modules:
  0.0 123.0 jit_solution(11380233408203592717)
XLA Ops:
  0.6 0.0 copy-start
  0.6 1.2 copy-done
  1.9 2.9 %fusion = f16[768,256]{1,0:T(8,128)(2,1)S(1)} fusion(bf16[768,2048]{1,0:T(8,128)(2,1)} %slab_ref.1, bf16[2048,256]{1,0:T(8,128)(2,1)S(1)} %copy-done), kind=kOutput, calls=%fused_computation.1 | convolution fusion | flops 805699584 | bytes 4587520 | tf_op jit(solution)/shard_map/sample/dot_general | solution.py:169
  4.7 16.7 %all_to_all.25 = f16[32,24,256]{2,1,0:T(8,128)(2,1)S(1)} all-to-all(f16[32,24,256]{2,1,0:T(8,128)(2,1)S(1)} %bitcast.18), channel_id=1, replica_groups=mesh['row'=16,'col'=32] {'col'}, dimensions={0} | all-to-all | bytes 786432 | tf_op jit(solution)/shard_map/sample/all_to_all | solution.py:171
  21.4 0.1 convert_reduce_fusion
  21.5 0.8 broadcast_in_dim.6
  22.3 5.8 %all-to-all-start.1 = ((f16[32,24,256]{2,1,0:T(8,128)(2,1)}), f16[32,24,256]{2,1,0:T(8,128)(2,1)S(1)}, u32[]{:S(2)}, u32[]{:S(2)}) async-start(f16[32,24,256]{2,1,0:T(8,128)(2,1)} %broadcast_in_dim.6), calls=%async_computation.1 | async-start | bytes 786432 | tf_op jit(solution)/shard_map/sample/all_to_all | solution.py:173
  28.1 8.0 %all-to-all-done.1 = f16[32,24,256]{2,1,0:T(8,128)(2,1)S(1)} async-done(((f16[32,24,256]{2,1,0:T(8,128)(2,1)}), f16[32,24,256]{2,1,0:T(8,128)(2,1)S(1)}, u32[]{:S(2)}, u32[]{:S(2)}) %all-to-all-start.1) | async-done | bytes 393248 | tf_op jit(solution)/shard_map/sample/all_to_all | solution.py:173
  36.1 1.5 %convolution_bitcast_fusion = f32[256,256]{1,0:T(8,128)S(1)} fusion(f16[32,24,256]{2,1,0:T(8,128)(2,1)S(1)} %all-to-all-done.1), kind=kOutput, calls=%fused_computation.2 | convolution fusion | flops 604372992 | bytes 655360 | tf_op jit(solution)/shard_map/gram/dot_general | solution.py:176
  37.6 0.7 broadcast_in_dim.7
  38.3 14.0 %all-to-all-start.2 = ((f32[16,8,256]{2,1,0:T(8,128)}), f32[16,8,256]{2,1,0:T(8,128)S(1)}, u32[]{:S(2)}, u32[]{:S(2)}) async-start(f32[16,8,256]{2,1,0:T(8,128)} %broadcast_in_dim.7), calls=%async_computation.2 | async-start | bytes 262144 | tf_op jit(solution)/shard_map/gram/all_to_all | solution.py:178
  52.3 0.1 convert_multiply_fusion
  52.4 0.5 copy.11
  52.9 4.3 %product_quarters.1 = (f32[256,512]{1,0:T(8,128)S(1)}, f32[256,512]{1,0:T(8,128)}, f32[256,512]{1,0:T(8,128)}, f32[128,512]{1,0:T(8,128)}, f32[128,512]{1,0:T(8,128)}) custom-call(f32[768,256]{1,0:T(8,128)S(1)} %bitcast.16, bf16[768,2048]{1,0:T(8,128)(2,1)} %slab_ref.1), custom_call_target="tpu_custom_call" | custom-call | flops 1600000000 | bytes 6291456 | tf_op jit(solution)/shard_map/product/product_quarters/pallas_call | solution.py:141
  57.2 3.8 %collective-permute-start = (f32[256,512]{1,0:T(8,128)}, f32[256,512]{1,0:T(8,128)S(1)}, u32[]{:S(2)}, u32[]{:S(2)}) collective-permute-start(f32[256,512]{1,0:T(8,128)} %get-tuple-element.14), channel_id=1, source_target_pairs={{0,32},{32,64},{64,96},{96,128},{128,160},{160,192},{192,224},{224... | collective-permute-start | bytes 1572872 | tf_op jit(solution)/shard_map/product/ppermute | solution.py:154
  61.0 3.2 %collective-permute-start.1 = (f32[256,512]{1,0:T(8,128)}, f32[256,512]{1,0:T(8,128)S(1)}, u32[]{:S(2)}, u32[]{:S(2)}) collective-permute-start(f32[256,512]{1,0:T(8,128)} %get-tuple-element.15), channel_id=1, source_target_pairs={{0,480},{32,0},{64,32},{96,64},{128,96},{160,128},{192,160},{224,1... | collective-permute-start | bytes 1572872 | tf_op jit(solution)/shard_map/product/ppermute | solution.py:154
  64.2 2.1 %all-to-all-done.2 = f32[16,8,256]{2,1,0:T(8,128)S(1)} async-done(((f32[16,8,256]{2,1,0:T(8,128)}), f32[16,8,256]{2,1,0:T(8,128)S(1)}, u32[]{:S(2)}, u32[]{:S(2)}) %all-to-all-start.2) | async-done | bytes 131104 | tf_op jit(solution)/shard_map/gram/all_to_all | solution.py:178
  66.4 0.7 broadcast_in_dim.8
  67.1 6.5 %all-to-all-start.3 = ((f32[32,8,256]{2,1,0:T(8,128)}), f32[32,8,256]{2,1,0:T(8,128)S(1)}, u32[]{:S(2)}, u32[]{:S(2)}) async-start(f32[32,8,256]{2,1,0:T(8,128)} %broadcast_in_dim.8), calls=%async_computation.3 | async-start | bytes 524288 | tf_op jit(solution)/shard_map/gram/all_to_all | solution.py:185
  73.6 4.1 %collective-permute-start.2 = (f32[128,512]{1,0:T(8,128)}, f32[128,512]{1,0:T(8,128)S(1)}, u32[]{:S(2)}, u32[]{:S(2)}) collective-permute-start(f32[128,512]{1,0:T(8,128)} %get-tuple-element.16), channel_id=1, source_target_pairs={{0,64},{32,96},{64,128},{96,160},{128,192},{160,224},{192,256},{22... | collective-permute-start | bytes 786440 | tf_op jit(solution)/shard_map/product/ppermute | solution.py:154
  77.7 4.0 %collective-permute-start.3 = (f32[128,512]{1,0:T(8,128)}, f32[128,512]{1,0:T(8,128)}, u32[]{:S(2)}, u32[]{:S(2)}) collective-permute-start(f32[128,512]{1,0:T(8,128)} %get-tuple-element.17), channel_id=1, source_target_pairs={{0,448},{32,480},{64,0},{96,32},{128,64},{160,96},{192,128},{224,1... | collective-permute-start | bytes 786440 | tf_op jit(solution)/shard_map/product/ppermute | solution.py:154
  81.7 0.0 all-to-all-done.3
  81.7 9.8 %inverse_factor.1.inv_ref = f32[256,256]{1,0:T(8,128)S(1)} custom-call(f32[256,256]{1,0:T(8,128)S(1)} %bitcast.15), custom_call_target="tpu_custom_call" | custom-call | flops 100000000 | bytes 1048576 | tf_op jit(solution)/shard_map/factor/inverse_factor/pallas_call | solution.py:82
  91.5 0.0 collective-permute-done.left_ref
  91.6 0.0 collective-permute-done.1.right_ref
  91.6 0.0 collective-permute-done.2.up_ref
  91.6 3.0 %collective-permute-done.3.down_ref = f32[128,512]{1,0:T(8,128)} collective-permute-done((f32[128,512]{1,0:T(8,128)}, f32[128,512]{1,0:T(8,128)}, u32[]{:S(2)}, u32[]{:S(2)}) %collective-permute-start.3) | collective-permute-done | bytes 262176 | tf_op jit(solution)/shard_map/product/ppermute | solution.py:154
  94.6 1.6 %apply_inverse.1 = f32[256,512]{1,0:T(8,128)S(1)} custom-call(f32[256,256]{1,0:T(8,128)S(1)} %inverse_factor.1.inv_ref, f32[256,512]{1,0:T(8,128)S(1)} %get-tuple-element.13.mine_ref, f32[256,512]{1,0:T(8,128)S(1)} %collective-permute-done.left_ref, f32[256,512]{1,0:T(8,128)S(1)} %collective-permute-done.1.right_ref, ...), custom_call_target="tpu_custom_call" | custom-call | flops 600000000 | bytes 3145728 | tf_op jit(solution)/shard_map/projected/apply_inverse/pallas_call | solution.py:100
  96.2 0.7 convert_element_type.32
  96.9 7.6 %all-to-all-start.4 = ((f16[16,16,512]{2,1,0:T(8,128)(2,1)}), f16[16,16,512]{2,1,0:T(8,128)(2,1)S(1)}, u32[]{:S(2)}, u32[]{:S(2)}) async-start(f16[16,16,512]{2,1,0:T(8,128)(2,1)} %bitcast.4), calls=%async_computation.4 | async-start | bytes 524288 | tf_op jit(solution)/shard_map/projected/all_to_all | solution.py:192
  104.5 0.9 fusion.1
  105.5 16.8 %all-to-all-done.4 = f16[16,16,512]{2,1,0:T(8,128)(2,1)S(1)} async-done(((f16[16,16,512]{2,1,0:T(8,128)(2,1)}), f16[16,16,512]{2,1,0:T(8,128)(2,1)S(1)}, u32[]{:S(2)}, u32[]{:S(2)}) %all-to-all-start.4) | async-done | bytes 262176 | tf_op jit(solution)/shard_map/projected/all_to_all | solution.py:192
  122.3 0.7 copy.13
  (5 shorter events, 0.1 us)
Async XLA Ops:
  0.6 1.2 %copy-start = (bf16[2048,256]{1,0:T(8,128)(2,1)S(1)}, bf16[2048,256]{1,0:T(8,128)(2,1)}, u32[]{:S(2)}) copy-start(bf16[2048,256]{1,0:T(8,128)(2,1)} %param.3) | copy-start | bytes 3145732
  22.3 13.8 %all-to-all-start.1 = ((f16[32,24,256]{2,1,0:T(8,128)(2,1)}), f16[32,24,256]{2,1,0:T(8,128)(2,1)S(1)}, u32[]{:S(2)}, u32[]{:S(2)}) async-start(f16[32,24,256]{2,1,0:T(8,128)(2,1)} %broadcast_in_dim.6), calls=%async_computation.1 | async-start | bytes 786432 | tf_op jit(solution)/shard_map/sample/all_to_all | solution.py:173
  38.3 28.0 %all-to-all-start.2 = ((f32[16,8,256]{2,1,0:T(8,128)}), f32[16,8,256]{2,1,0:T(8,128)S(1)}, u32[]{:S(2)}, u32[]{:S(2)}) async-start(f32[16,8,256]{2,1,0:T(8,128)} %broadcast_in_dim.7), calls=%async_computation.2 | async-start | bytes 262144 | tf_op jit(solution)/shard_map/gram/all_to_all | solution.py:178
  57.2 34.4 %collective-permute-start = (f32[256,512]{1,0:T(8,128)}, f32[256,512]{1,0:T(8,128)S(1)}, u32[]{:S(2)}, u32[]{:S(2)}) collective-permute-start(f32[256,512]{1,0:T(8,128)} %get-tuple-element.14), channel_id=1, source_target_pairs={{0,32},{32,64},{64,96},{96,128},{128,160},{160,192},{192,224},{224... | collective-permute-start | bytes 1572872 | tf_op jit(solution)/shard_map/product/ppermute | solution.py:154
  61.0 30.5 %collective-permute-start.1 = (f32[256,512]{1,0:T(8,128)}, f32[256,512]{1,0:T(8,128)S(1)}, u32[]{:S(2)}, u32[]{:S(2)}) collective-permute-start(f32[256,512]{1,0:T(8,128)} %get-tuple-element.15), channel_id=1, source_target_pairs={{0,480},{32,0},{64,32},{96,64},{128,96},{160,128},{192,160},{224,1... | collective-permute-start | bytes 1572872 | tf_op jit(solution)/shard_map/product/ppermute | solution.py:154
  67.1 14.6 %all-to-all-start.3 = ((f32[32,8,256]{2,1,0:T(8,128)}), f32[32,8,256]{2,1,0:T(8,128)S(1)}, u32[]{:S(2)}, u32[]{:S(2)}) async-start(f32[32,8,256]{2,1,0:T(8,128)} %broadcast_in_dim.8), calls=%async_computation.3 | async-start | bytes 524288 | tf_op jit(solution)/shard_map/gram/all_to_all | solution.py:185
  73.6 18.0 %collective-permute-start.2 = (f32[128,512]{1,0:T(8,128)}, f32[128,512]{1,0:T(8,128)S(1)}, u32[]{:S(2)}, u32[]{:S(2)}) collective-permute-start(f32[128,512]{1,0:T(8,128)} %get-tuple-element.16), channel_id=1, source_target_pairs={{0,64},{32,96},{64,128},{96,160},{128,192},{160,224},{192,256},{22... | collective-permute-start | bytes 786440 | tf_op jit(solution)/shard_map/product/ppermute | solution.py:154
  77.7 16.9 %collective-permute-start.3 = (f32[128,512]{1,0:T(8,128)}, f32[128,512]{1,0:T(8,128)}, u32[]{:S(2)}, u32[]{:S(2)}) collective-permute-start(f32[128,512]{1,0:T(8,128)} %get-tuple-element.17), channel_id=1, source_target_pairs={{0,448},{32,480},{64,0},{96,32},{128,64},{160,96},{192,128},{224,1... | collective-permute-start | bytes 786440 | tf_op jit(solution)/shard_map/product/ppermute | solution.py:154
  96.9 25.3 %all-to-all-start.4 = ((f16[16,16,512]{2,1,0:T(8,128)(2,1)}), f16[16,16,512]{2,1,0:T(8,128)(2,1)S(1)}, u32[]{:S(2)}, u32[]{:S(2)}) async-start(f16[16,16,512]{2,1,0:T(8,128)(2,1)} %bitcast.4), calls=%async_computation.4 | async-start | bytes 524288 | tf_op jit(solution)/shard_map/projected/all_to_all | solution.py:192

commit v5 on v4

--- a/solution.py
+++ b/solution.py
@@ -33,19 +33,18 @@
             a, b, c = s[k][k], s[k + 1][k], s[k + 1][k + 1]
             det = a * c - b * b
             inv = 1.0 / det
-            pa, pb, pc = a * inv, b * inv, c * inv
             for i in range(k + 2, 8):
-                m0 = pc * s[i][k] - pb * s[i][k + 1]
-                m1 = pa * s[i][k + 1] - pb * s[i][k]
+                u0 = c * s[i][k] - b * s[i][k + 1]
+                u1 = a * s[i][k + 1] - b * s[i][k]
                 for m in range(k + 2, i + 1):
-                    s[i][m] = s[i][m] - (m0 * s[m][k] + m1 * s[m][k + 1])
-                rows[i] = rows[i] - (m0 * rows[k] + m1 * rows[k + 1])
+                    s[i][m] = s[i][m] - inv * (u0 * s[m][k] + u1 * s[m][k + 1])
+                rows[i] = rows[i] - inv * (u0 * rows[k] + u1 * rows[k + 1])
             for h in later:
-                m0 = pc * cols[h][k] - pb * cols[h][k + 1]
-                m1 = pa * cols[h][k + 1] - pb * cols[h][k]
+                u0 = inv * (c * cols[h][k] - b * cols[h][k + 1])
+                u1 = inv * (a * cols[h][k + 1] - b * cols[h][k])
                 for m in range(k + 2, 8):
-                    cols[h][m] = cols[h][m] - (m0 * s[m][k] + m1 * s[m][k + 1])
-                groups[h] = groups[h] - (m0 * rows[k] + m1 * rows[k + 1])
+                    cols[h][m] = cols[h][m] - (u0 * s[m][k] + u1 * s[m][k + 1])
+                groups[h] = groups[h] - (u0 * rows[k] + u1 * rows[k + 1])
             inv_a = 1.0 / a
             x0 = rows[k] * lax.rsqrt(a)
             x1 = (rows[k + 1] - (b * inv_a) * rows[k]) * lax.rsqrt(det * inv_a)
@@ -89,17 +88,26 @@
     )(gram)
 
 
-def apply_kernel(inv_ref, mine_ref, left_ref, right_ref, up_ref, down_ref, proj_ref):
-    half = up_ref.shape[0]
+def apply_kernel(inv_ref, mine_ref, left_ref, right_ref, up_ref, down_ref, proj_ref, down, sem):
+    load = pltpu.make_async_copy(down_ref, down, sem)
+    load.start()
+    split = up_ref.shape[0]
     near = mine_ref[...] + left_ref[...] + right_ref[...]
-    total = jnp.concatenate([near[:half] + up_ref[...], near[half:] + down_ref[...]], axis=0)
-    proj_ref[...] = jnp.dot(inv_ref[...], total, precision=EXACT, preferred_element_type=F32) * PROJ_SCALE
+    upper = near[:split] + up_ref[...]
+    first = jnp.dot(inv_ref[:, :split], upper, precision=EXACT, preferred_element_type=F32)
+    load.wait()
+    rest = near[split:] + down[...]
+    second = jnp.dot(inv_ref[:, split:], rest, precision=EXACT, preferred_element_type=F32)
+    proj_ref[...] = (first + second) * PROJ_SCALE
 
 
 def apply_inverse(inverse, parts):
+    whole, last = pl.BlockSpec(memory_space=pltpu.VMEM), parts[-1]
     return pl.pallas_call(
         apply_kernel,
         out_shape=jax.ShapeDtypeStruct(parts[0].shape, F32),
+        in_specs=[whole] * len(parts) + [pl.BlockSpec(memory_space=pl.ANY)],
+        scratch_shapes=[pltpu.VMEM(last.shape, F32), pltpu.SemaphoreType.DMA],
         compiler_params=pltpu.CompilerParams(vmem_limit_bytes=16 * 2**20),
         cost_estimate=pl.CostEstimate(flops=6 * 10**8, bytes_accessed=3 * 2**20, transcendentals=0),
         name="apply_inverse",
@@ -107,7 +115,7 @@
 
 
 def product_kernel(sampled_ref, slab_ref, mine_ref, right_ref, left_ref, far_up_ref, far_down_ref, held, sems):
-    half, width = far_up_ref.shape
+    split, width = far_up_ref.shape
     at = lax.axis_index("row")
 
     def load(step):
@@ -129,18 +137,19 @@
     right_ref[...] = quarter(1)
     left_ref[...] = quarter(GROUP - 1)
     far = quarter(2)
-    far_up_ref[...] = far[:half]
-    far_down_ref[...] = far[half:]
+    far_up_ref[...] = far[:split]
+    far_down_ref[...] = far[split:]
     mine_ref[...] = quarter(0)
 
 
 def product_quarters(sampled, slab):
     (rows, n), width = sampled.shape, slab.shape[1] // GROUP
     whole = jax.ShapeDtypeStruct((n, width), F32)
-    part = jax.ShapeDtypeStruct((n // 2, width), F32)
+    upper = jax.ShapeDtypeStruct((n // 2, width), F32)
+    lower = jax.ShapeDtypeStruct((n // 2, width), F32)
     return pl.pallas_call(
         product_kernel,
-        out_shape=(whole, whole, whole, part, part),
+        out_shape=(whole, whole, whole, upper, lower),
         in_specs=[pl.BlockSpec(memory_space=pltpu.VMEM), pl.BlockSpec(memory_space=pl.ANY)],
         scratch_shapes=[pltpu.VMEM((GROUP, rows, width), slab.dtype), pltpu.SemaphoreType.DMA((GROUP,))],
         compiler_params=pltpu.CompilerParams(vmem_limit_bytes=PRODUCT_MIB * 2**20),

time: 124 us -> 124 us (level)
  no operation moved by 1% of the time
where the time goes in v5:
time: 124 us; the launch traced here: 123 us
  starting transfers between devices  49 us (40%)
  waiting for transfers between devices  30.6 us (25%)
  blocking collectives  16.7 us (13%)
  Pallas kernels  15.4 us (12%)
  matrix products  5.3 us (4%)
  local copies, waits for them, and re-layouts  4.51 us (4%)
    all_to_all x1, waiting for transfers between devices, local(): lax.all_to_all(sent, 'row', 0, 0)  16.8 us
    all_to_all x1, blocking collectives, local(): got = lax.all_to_all(sent, 'col', 0, 0)  16.7 us
    ppermute x4, starting transfers between devices, shift(): return lax.ppermute(x, 'row', [(i, (i + step) % size) for i in range(size)])  15.2 us
    all_to_all x1, starting transfers between devices, local(): strip = jnp.sum(lax.all_to_all(copies(part, row_size), 'row', 0, 0), axis=0)  14 us
    pallas_call x1, Pallas kernels, inverse_factor(): pl.pallas_call(factor_kernel, out_shape=jax.ShapeDtypeStruct((n, n), F32)...  9.18 us
    all_to_all x1, waiting for transfers between devices, local(): lax.all_to_all(copies((own * SAMPLE_SCALE).astype(F16), col_size), 'col',...  8.04 us
    all_to_all x1, starting transfers between devices, local(): lax.all_to_all(sent, 'row', 0, 0)  7.58 us
    all_to_all x1, starting transfers between devices, local(): lax.all_to_all(copies(strip, col_size), 'col', 0, 0).reshape(width, width)  6.49 us
  transfers between devices with their start and end apart: 8, of which 4 were waited for; matrix products, arithmetic and copies ran while one was open for 2% of the time, Pallas kernels for 11%

profile of v5, /device:TPU:6, one launch (start us, length us, event | category | flops | bytes accessed | tf_op | source)
XLA Modules:
  0.0 123.3 jit_solution(3563120637491724563)
XLA Ops:
  0.6 0.0 copy-start
  0.6 1.2 copy-done
  1.9 2.9 %fusion = f16[768,256]{1,0:T(8,128)(2,1)S(1)} fusion(bf16[768,2048]{1,0:T(8,128)(2,1)} %slab_ref.1, bf16[2048,256]{1,0:T(8,128)(2,1)S(1)} %copy-done), kind=kOutput, calls=%fused_computation.1 | convolution fusion | flops 805699584 | bytes 4587520 | tf_op jit(solution)/shard_map/sample/dot_general | solution.py:178
  4.7 16.7 %all_to_all.25 = f16[32,24,256]{2,1,0:T(8,128)(2,1)S(1)} all-to-all(f16[32,24,256]{2,1,0:T(8,128)(2,1)S(1)} %bitcast.18), channel_id=1, replica_groups=mesh['row'=16,'col'=32] {'col'}, dimensions={0} | all-to-all | bytes 786432 | tf_op jit(solution)/shard_map/sample/all_to_all | solution.py:180
  21.4 0.1 convert_reduce_fusion
  21.5 0.8 broadcast_in_dim.6
  22.3 5.8 %all-to-all-start.1 = ((f16[32,24,256]{2,1,0:T(8,128)(2,1)}), f16[32,24,256]{2,1,0:T(8,128)(2,1)S(1)}, u32[]{:S(2)}, u32[]{:S(2)}) async-start(f16[32,24,256]{2,1,0:T(8,128)(2,1)} %broadcast_in_dim.6), calls=%async_computation.1 | async-start | bytes 786432 | tf_op jit(solution)/shard_map/sample/all_to_all | solution.py:182
  28.1 8.0 %all-to-all-done.1 = f16[32,24,256]{2,1,0:T(8,128)(2,1)S(1)} async-done(((f16[32,24,256]{2,1,0:T(8,128)(2,1)}), f16[32,24,256]{2,1,0:T(8,128)(2,1)S(1)}, u32[]{:S(2)}, u32[]{:S(2)}) %all-to-all-start.1) | async-done | bytes 393248 | tf_op jit(solution)/shard_map/sample/all_to_all | solution.py:182
  36.1 1.5 %convolution_bitcast_fusion = f32[256,256]{1,0:T(8,128)S(1)} fusion(f16[32,24,256]{2,1,0:T(8,128)(2,1)S(1)} %all-to-all-done.1), kind=kOutput, calls=%fused_computation.2 | convolution fusion | flops 604372992 | bytes 655360 | tf_op jit(solution)/shard_map/gram/dot_general | solution.py:185
  37.6 0.7 broadcast_in_dim.7
  38.3 14.0 %all-to-all-start.2 = ((f32[16,8,256]{2,1,0:T(8,128)}), f32[16,8,256]{2,1,0:T(8,128)S(1)}, u32[]{:S(2)}, u32[]{:S(2)}) async-start(f32[16,8,256]{2,1,0:T(8,128)} %broadcast_in_dim.7), calls=%async_computation.2 | async-start | bytes 262144 | tf_op jit(solution)/shard_map/gram/all_to_all | solution.py:187
  52.3 0.1 convert_multiply_fusion
  52.4 0.5 copy.11
  52.9 4.3 %product_quarters.1 = (f32[256,512]{1,0:T(8,128)S(1)}, f32[256,512]{1,0:T(8,128)}, f32[256,512]{1,0:T(8,128)}, f32[128,512]{1,0:T(8,128)}, f32[128,512]{1,0:T(8,128)}) custom-call(f32[768,256]{1,0:T(8,128)S(1)} %bitcast.16, bf16[768,2048]{1,0:T(8,128)(2,1)} %slab_ref.1), custom_call_target="tpu_custom_call" | custom-call | flops 1600000000 | bytes 6291456 | tf_op jit(solution)/shard_map/product/product_quarters/pallas_call | solution.py:150
  57.2 3.8 %collective-permute-start = (f32[256,512]{1,0:T(8,128)}, f32[256,512]{1,0:T(8,128)S(1)}, u32[]{:S(2)}, u32[]{:S(2)}) collective-permute-start(f32[256,512]{1,0:T(8,128)} %get-tuple-element.14), channel_id=1, source_target_pairs={{0,32},{32,64},{64,96},{96,128},{128,160},{160,192},{192,224},{224... | collective-permute-start | bytes 1572872 | tf_op jit(solution)/shard_map/product/ppermute | solution.py:163
  61.0 3.2 %collective-permute-start.1 = (f32[256,512]{1,0:T(8,128)}, f32[256,512]{1,0:T(8,128)S(1)}, u32[]{:S(2)}, u32[]{:S(2)}) collective-permute-start(f32[256,512]{1,0:T(8,128)} %get-tuple-element.15), channel_id=1, source_target_pairs={{0,480},{32,0},{64,32},{96,64},{128,96},{160,128},{192,160},{224,1... | collective-permute-start | bytes 1572872 | tf_op jit(solution)/shard_map/product/ppermute | solution.py:163
  64.2 2.1 %all-to-all-done.2 = f32[16,8,256]{2,1,0:T(8,128)S(1)} async-done(((f32[16,8,256]{2,1,0:T(8,128)}), f32[16,8,256]{2,1,0:T(8,128)S(1)}, u32[]{:S(2)}, u32[]{:S(2)}) %all-to-all-start.2) | async-done | bytes 131104 | tf_op jit(solution)/shard_map/gram/all_to_all | solution.py:187
  66.4 0.7 broadcast_in_dim.8
  67.1 6.5 %all-to-all-start.3 = ((f32[32,8,256]{2,1,0:T(8,128)}), f32[32,8,256]{2,1,0:T(8,128)S(1)}, u32[]{:S(2)}, u32[]{:S(2)}) async-start(f32[32,8,256]{2,1,0:T(8,128)} %broadcast_in_dim.8), calls=%async_computation.3 | async-start | bytes 524288 | tf_op jit(solution)/shard_map/gram/all_to_all | solution.py:194
  73.6 4.1 %collective-permute-start.2 = (f32[128,512]{1,0:T(8,128)}, f32[128,512]{1,0:T(8,128)S(1)}, u32[]{:S(2)}, u32[]{:S(2)}) collective-permute-start(f32[128,512]{1,0:T(8,128)} %get-tuple-element.16), channel_id=1, source_target_pairs={{0,64},{32,96},{64,128},{96,160},{128,192},{160,224},{192,256},{22... | collective-permute-start | bytes 786440 | tf_op jit(solution)/shard_map/product/ppermute | solution.py:163
  77.7 4.0 %collective-permute-start.3 = (f32[128,512]{1,0:T(8,128)}, f32[128,512]{1,0:T(8,128)}, u32[]{:S(2)}, u32[]{:S(2)}) collective-permute-start(f32[128,512]{1,0:T(8,128)} %get-tuple-element.17), channel_id=1, source_target_pairs={{0,448},{32,480},{64,0},{96,32},{128,64},{160,96},{192,128},{224,1... | collective-permute-start | bytes 786440 | tf_op jit(solution)/shard_map/product/ppermute | solution.py:163
  81.7 0.0 all-to-all-done.3
  81.7 9.2 %inverse_factor.1.inv_ref = f32[256,256]{1,0:T(8,128)S(1)} custom-call(f32[256,256]{1,0:T(8,128)S(1)} %bitcast.15), custom_call_target="tpu_custom_call" | custom-call | flops 100000000 | bytes 1048576 | tf_op jit(solution)/shard_map/factor/inverse_factor/pallas_call | solution.py:81
  90.9 0.0 collective-permute-done.left_ref
  90.9 0.0 collective-permute-done.1.right_ref
  90.9 0.0 collective-permute-done.2.up_ref
  91.0 3.6 %collective-permute-done.3.down_ref = f32[128,512]{1,0:T(8,128)} collective-permute-done((f32[128,512]{1,0:T(8,128)}, f32[128,512]{1,0:T(8,128)}, u32[]{:S(2)}, u32[]{:S(2)}) %collective-permute-start.3) | collective-permute-done | bytes 262176 | tf_op jit(solution)/shard_map/product/ppermute | solution.py:163
  94.6 2.0 %apply_inverse.1 = f32[256,512]{1,0:T(8,128)S(1)} custom-call(f32[256,256]{1,0:T(8,128)S(1)} %inverse_factor.1.inv_ref, f32[256,512]{1,0:T(8,128)S(1)} %get-tuple-element.13.mine_ref, f32[256,512]{1,0:T(8,128)S(1)} %collective-permute-done.left_ref, f32[256,512]{1,0:T(8,128)S(1)} %collective-permute-done.1.right_ref, ...), custom_call_target="tpu_custom_call" | custom-call | flops 600000000 | bytes 3145728 | tf_op jit(solution)/shard_map/projected/apply_inverse/pallas_call | solution.py:106
  96.5 0.7 convert_element_type.32
  97.3 7.6 %all-to-all-start.4 = ((f16[16,16,512]{2,1,0:T(8,128)(2,1)}), f16[16,16,512]{2,1,0:T(8,128)(2,1)S(1)}, u32[]{:S(2)}, u32[]{:S(2)}) async-start(f16[16,16,512]{2,1,0:T(8,128)(2,1)} %bitcast.4), calls=%async_computation.4 | async-start | bytes 524288 | tf_op jit(solution)/shard_map/projected/all_to_all | solution.py:201
  104.9 0.9 fusion.1
  105.8 16.8 %all-to-all-done.4 = f16[16,16,512]{2,1,0:T(8,128)(2,1)S(1)} async-done(((f16[16,16,512]{2,1,0:T(8,128)(2,1)}), f16[16,16,512]{2,1,0:T(8,128)(2,1)S(1)}, u32[]{:S(2)}, u32[]{:S(2)}) %all-to-all-start.4) | async-done | bytes 262176 | tf_op jit(solution)/shard_map/projected/all_to_all | solution.py:201
  122.7 0.7 copy.13
  (5 shorter events, 0.1 us)
Async XLA Ops:
  0.6 1.2 copy-start
  22.3 13.8 %all-to-all-start.1 = ((f16[32,24,256]{2,1,0:T(8,128)(2,1)}), f16[32,24,256]{2,1,0:T(8,128)(2,1)S(1)}, u32[]{:S(2)}, u32[]{:S(2)}) async-start(f16[32,24,256]{2,1,0:T(8,128)(2,1)} %broadcast_in_dim.6), calls=%async_computation.1 | async-start | bytes 786432 | tf_op jit(solution)/shard_map/sample/all_to_all | solution.py:182
  38.3 28.0 %all-to-all-start.2 = ((f32[16,8,256]{2,1,0:T(8,128)}), f32[16,8,256]{2,1,0:T(8,128)S(1)}, u32[]{:S(2)}, u32[]{:S(2)}) async-start(f32[16,8,256]{2,1,0:T(8,128)} %broadcast_in_dim.7), calls=%async_computation.2 | async-start | bytes 262144 | tf_op jit(solution)/shard_map/gram/all_to_all | solution.py:187
  57.2 33.8 %collective-permute-start = (f32[256,512]{1,0:T(8,128)}, f32[256,512]{1,0:T(8,128)S(1)}, u32[]{:S(2)}, u32[]{:S(2)}) collective-permute-start(f32[256,512]{1,0:T(8,128)} %get-tuple-element.14), channel_id=1, source_target_pairs={{0,32},{32,64},{64,96},{96,128},{128,160},{160,192},{192,224},{224... | collective-permute-start | bytes 1572872 | tf_op jit(solution)/shard_map/product/ppermute | solution.py:163
  61.0 29.9 %collective-permute-start.1 = (f32[256,512]{1,0:T(8,128)}, f32[256,512]{1,0:T(8,128)S(1)}, u32[]{:S(2)}, u32[]{:S(2)}) collective-permute-start(f32[256,512]{1,0:T(8,128)} %get-tuple-element.15), channel_id=1, source_target_pairs={{0,480},{32,0},{64,32},{96,64},{128,96},{160,128},{192,160},{224,1... | collective-permute-start | bytes 1572872 | tf_op jit(solution)/shard_map/product/ppermute | solution.py:163
  67.1 14.6 %all-to-all-start.3 = ((f32[32,8,256]{2,1,0:T(8,128)}), f32[32,8,256]{2,1,0:T(8,128)S(1)}, u32[]{:S(2)}, u32[]{:S(2)}) async-start(f32[32,8,256]{2,1,0:T(8,128)} %broadcast_in_dim.8), calls=%async_computation.3 | async-start | bytes 524288 | tf_op jit(solution)/shard_map/gram/all_to_all | solution.py:194
  73.6 17.4 %collective-permute-start.2 = (f32[128,512]{1,0:T(8,128)}, f32[128,512]{1,0:T(8,128)S(1)}, u32[]{:S(2)}, u32[]{:S(2)}) collective-permute-start(f32[128,512]{1,0:T(8,128)} %get-tuple-element.16), channel_id=1, source_target_pairs={{0,64},{32,96},{64,128},{96,160},{128,192},{160,224},{192,256},{22... | collective-permute-start | bytes 786440 | tf_op jit(solution)/shard_map/product/ppermute | solution.py:163
  77.7 16.9 %collective-permute-start.3 = (f32[128,512]{1,0:T(8,128)}, f32[128,512]{1,0:T(8,128)}, u32[]{:S(2)}, u32[]{:S(2)}) collective-permute-start(f32[128,512]{1,0:T(8,128)} %get-tuple-element.17), channel_id=1, source_target_pairs={{0,448},{32,480},{64,0},{96,32},{128,64},{160,96},{192,128},{224,1... | collective-permute-start | bytes 786440 | tf_op jit(solution)/shard_map/product/ppermute | solution.py:163
  97.3 25.3 %all-to-all-start.4 = ((f16[16,16,512]{2,1,0:T(8,128)(2,1)}), f16[16,16,512]{2,1,0:T(8,128)(2,1)S(1)}, u32[]{:S(2)}, u32[]{:S(2)}) async-start(f16[16,16,512]{2,1,0:T(8,128)(2,1)} %bitcast.4), calls=%async_computation.4 | async-start | bytes 524288 | tf_op jit(solution)/shard_map/projected/all_to_all | solution.py:201

commit v6 on v5

--- a/solution.py
+++ b/solution.py
@@ -83,31 +83,22 @@
         out_shape=jax.ShapeDtypeStruct((n, n), F32),
         scratch_shapes=[pltpu.VMEM((n, 2 * n), F32), pltpu.VMEM((TILE, 2 * TILE), F32)],
         compiler_params=pltpu.CompilerParams(vmem_limit_bytes=16 * 2**20),
-        cost_estimate=pl.CostEstimate(flops=10**8, bytes_accessed=2**20, transcendentals=0),
+        cost_estimate=pl.CostEstimate(flops=10**9, bytes_accessed=2**20, transcendentals=0),
         name="inverse_factor",
     )(gram)
 
 
-def apply_kernel(inv_ref, mine_ref, left_ref, right_ref, up_ref, down_ref, proj_ref, down, sem):
-    load = pltpu.make_async_copy(down_ref, down, sem)
-    load.start()
+def apply_kernel(inv_ref, mine_ref, left_ref, right_ref, up_ref, down_ref, proj_ref):
     split = up_ref.shape[0]
     near = mine_ref[...] + left_ref[...] + right_ref[...]
-    upper = near[:split] + up_ref[...]
-    first = jnp.dot(inv_ref[:, :split], upper, precision=EXACT, preferred_element_type=F32)
-    load.wait()
-    rest = near[split:] + down[...]
-    second = jnp.dot(inv_ref[:, split:], rest, precision=EXACT, preferred_element_type=F32)
-    proj_ref[...] = (first + second) * PROJ_SCALE
+    total = jnp.concatenate([near[:split] + up_ref[...], near[split:] + down_ref[...]], axis=0)
+    proj_ref[...] = jnp.dot(inv_ref[...], total, precision=EXACT, preferred_element_type=F32) * PROJ_SCALE
 
 
 def apply_inverse(inverse, parts):
-    whole, last = pl.BlockSpec(memory_space=pltpu.VMEM), parts[-1]
     return pl.pallas_call(
         apply_kernel,
         out_shape=jax.ShapeDtypeStruct(parts[0].shape, F32),
-        in_specs=[whole] * len(parts) + [pl.BlockSpec(memory_space=pl.ANY)],
-        scratch_shapes=[pltpu.VMEM(last.shape, F32), pltpu.SemaphoreType.DMA],
         compiler_params=pltpu.CompilerParams(vmem_limit_bytes=16 * 2**20),
         cost_estimate=pl.CostEstimate(flops=6 * 10**8, bytes_accessed=3 * 2**20, transcendentals=0),
         name="apply_inverse",
@@ -145,8 +136,8 @@
 def product_quarters(sampled, slab):
     (rows, n), width = sampled.shape, slab.shape[1] // GROUP
     whole = jax.ShapeDtypeStruct((n, width), F32)
-    upper = jax.ShapeDtypeStruct((n // 2, width), F32)
-    lower = jax.ShapeDtypeStruct((n // 2, width), F32)
+    upper = jax.ShapeDtypeStruct((n * 5 // 8, width), F32)
+    lower = jax.ShapeDtypeStruct((n * 3 // 8, width), F32)
     return pl.pallas_call(
         product_kernel,
         out_shape=(whole, whole, whole, upper, lower),

time: 124 us -> 126 us (1.016)
  starting transfers between devices: 49 us -> 51.9 us
  waiting for transfers between devices: 30.6 us -> 29 us
    all_to_all x1, starting transfers between devices: 7.58 us -> 10.4 us  [local(): lax.all_to_all(sent, 'row', 0, 0)]
    ppermute x4, waiting for transfers between devices: 3.63 us -> 1.96 us  [shift(): return lax.ppermute(x, 'row', [(i, (i + step) % size) for i in range(size)])]
  transfers between devices with their start and end apart: 8 -> 8, of which waited for: 4 -> 5; matrix products, arithmetic and copies ran while one was open for 2% -> 2% of each run, Pallas kernels for 11% -> 11%
where the time goes in v6:
time: 126 us; the launch traced here: 125 us
  starting transfers between devices  51.9 us (41%)
  waiting for transfers between devices  29 us (23%)
  blocking collectives  16.7 us (13%)
  Pallas kernels  14.9 us (12%)
  matrix products  5.3 us (4%)
  local copies, waits for them, and re-layouts  5.27 us (4%)
    all_to_all x1, waiting for transfers between devices, local(): lax.all_to_all(sent, 'row', 0, 0)  17.5 us
    all_to_all x1, blocking collectives, local(): got = lax.all_to_all(sent, 'col', 0, 0)  16.7 us
    ppermute x4, starting transfers between devices, shift(): return lax.ppermute(x, 'row', [(i, (i + step) % size) for i in range(size)])  15.2 us
    all_to_all x1, starting transfers between devices, local(): strip = jnp.sum(lax.all_to_all(copies(part, row_size), 'row', 0, 0), axis=0)  14 us
    all_to_all x1, starting transfers between devices, local(): lax.all_to_all(sent, 'row', 0, 0)  10.4 us
    pallas_call x1, Pallas kernels, inverse_factor(): pl.pallas_call(factor_kernel, out_shape=jax.ShapeDtypeStruct((n, n), F32)...  9.19 us
    all_to_all x1, waiting for transfers between devices, local(): lax.all_to_all(copies((own * SAMPLE_SCALE).astype(F16), col_size), 'col',...  8.04 us
    all_to_all x1, starting transfers between devices, local(): lax.all_to_all(copies(strip, col_size), 'col', 0, 0).reshape(width, width)  6.49 us
  transfers between devices with their start and end apart: 8, of which 5 were waited for; matrix products, arithmetic and copies ran while one was open for 2% of the time, Pallas kernels for 11%

profile of v6, /device:TPU:6, one launch (start us, length us, event | category | flops | bytes accessed | tf_op | source)
XLA Modules:
  0.0 124.8 jit_solution(17130386316237838284)
XLA Ops:
  0.6 0.0 copy-start
  0.6 1.2 copy-done
  1.9 2.9 %fusion = f16[768,256]{1,0:T(8,128)(2,1)S(1)} fusion(bf16[768,2048]{1,0:T(8,128)(2,1)} %slab_ref.1, bf16[2048,256]{1,0:T(8,128)(2,1)S(1)} %copy-done), kind=kOutput, calls=%fused_computation.1 | convolution fusion | flops 805699584 | bytes 4587520 | tf_op jit(solution)/shard_map/sample/dot_general | solution.py:169
  4.7 16.7 %all_to_all.25 = f16[32,24,256]{2,1,0:T(8,128)(2,1)S(1)} all-to-all(f16[32,24,256]{2,1,0:T(8,128)(2,1)S(1)} %bitcast.18), channel_id=1, replica_groups=mesh['row'=16,'col'=32] {'col'}, dimensions={0} | all-to-all | bytes 786432 | tf_op jit(solution)/shard_map/sample/all_to_all | solution.py:171
  21.4 0.1 convert_reduce_fusion
  21.5 0.8 broadcast_in_dim.6
  22.3 5.8 %all-to-all-start.1 = ((f16[32,24,256]{2,1,0:T(8,128)(2,1)}), f16[32,24,256]{2,1,0:T(8,128)(2,1)S(1)}, u32[]{:S(2)}, u32[]{:S(2)}) async-start(f16[32,24,256]{2,1,0:T(8,128)(2,1)} %broadcast_in_dim.6), calls=%async_computation.1 | async-start | bytes 786432 | tf_op jit(solution)/shard_map/sample/all_to_all | solution.py:173
  28.1 8.0 %all-to-all-done.1 = f16[32,24,256]{2,1,0:T(8,128)(2,1)S(1)} async-done(((f16[32,24,256]{2,1,0:T(8,128)(2,1)}), f16[32,24,256]{2,1,0:T(8,128)(2,1)S(1)}, u32[]{:S(2)}, u32[]{:S(2)}) %all-to-all-start.1) | async-done | bytes 393248 | tf_op jit(solution)/shard_map/sample/all_to_all | solution.py:173
  36.1 1.5 %convolution_bitcast_fusion = f32[256,256]{1,0:T(8,128)S(1)} fusion(f16[32,24,256]{2,1,0:T(8,128)(2,1)S(1)} %all-to-all-done.1), kind=kOutput, calls=%fused_computation.2 | convolution fusion | flops 604372992 | bytes 655360 | tf_op jit(solution)/shard_map/gram/dot_general | solution.py:176
  37.7 0.7 broadcast_in_dim.7
  38.3 14.0 %all-to-all-start.2 = ((f32[16,8,256]{2,1,0:T(8,128)}), f32[16,8,256]{2,1,0:T(8,128)S(1)}, u32[]{:S(2)}, u32[]{:S(2)}) async-start(f32[16,8,256]{2,1,0:T(8,128)} %broadcast_in_dim.7), calls=%async_computation.2 | async-start | bytes 262144 | tf_op jit(solution)/shard_map/gram/all_to_all | solution.py:178
  52.3 0.1 convert_multiply_fusion
  52.4 0.5 copy.11
  52.9 4.1 %product_quarters.1 = (f32[256,512]{1,0:T(8,128)S(1)}, f32[256,512]{1,0:T(8,128)}, f32[256,512]{1,0:T(8,128)}, f32[160,512]{1,0:T(8,128)S(1)}, f32[96,512]{1,0:T(8,128)}) custom-call(f32[768,256]{1,0:T(8,128)S(1)} %bitcast.15, bf16[768,2048]{1,0:T(8,128)(2,1)} %slab_ref.1), custom_call_target="tpu_custom_call" | custom-call | flops 1600000000 | bytes 6291456 | tf_op jit(solution)/shard_map/product/product_quarters/pallas_call | solution.py:141
  57.1 0.0 copy-start.1
  57.1 0.7 copy-done.1
  57.8 3.8 %collective-permute-start = (f32[256,512]{1,0:T(8,128)}, f32[256,512]{1,0:T(8,128)S(1)}, u32[]{:S(2)}, u32[]{:S(2)}) collective-permute-start(f32[256,512]{1,0:T(8,128)} %get-tuple-element.14), channel_id=1, source_target_pairs={{0,32},{32,64},{64,96},{96,128},{128,160},{160,192},{192,224},{224... | collective-permute-start | bytes 1572872 | tf_op jit(solution)/shard_map/product/ppermute | solution.py:154
  61.6 3.2 %collective-permute-start.1 = (f32[256,512]{1,0:T(8,128)}, f32[256,512]{1,0:T(8,128)S(1)}, u32[]{:S(2)}, u32[]{:S(2)}) collective-permute-start(f32[256,512]{1,0:T(8,128)} %get-tuple-element.15), channel_id=1, source_target_pairs={{0,480},{32,0},{64,32},{96,64},{128,96},{160,128},{192,160},{224,1... | collective-permute-start | bytes 1572872 | tf_op jit(solution)/shard_map/product/ppermute | solution.py:154
  64.9 1.5 %all-to-all-done.2 = f32[16,8,256]{2,1,0:T(8,128)S(1)} async-done(((f32[16,8,256]{2,1,0:T(8,128)}), f32[16,8,256]{2,1,0:T(8,128)S(1)}, u32[]{:S(2)}, u32[]{:S(2)}) %all-to-all-start.2) | async-done | bytes 131104 | tf_op jit(solution)/shard_map/gram/all_to_all | solution.py:178
  66.4 0.7 broadcast_in_dim.8
  67.1 6.5 %all-to-all-start.3 = ((f32[32,8,256]{2,1,0:T(8,128)}), f32[32,8,256]{2,1,0:T(8,128)S(1)}, u32[]{:S(2)}, u32[]{:S(2)}) async-start(f32[32,8,256]{2,1,0:T(8,128)} %broadcast_in_dim.8), calls=%async_computation.3 | async-start | bytes 524288 | tf_op jit(solution)/shard_map/gram/all_to_all | solution.py:185
  73.6 4.1 %collective-permute-start.2 = (f32[160,512]{1,0:T(8,128)}, f32[160,512]{1,0:T(8,128)S(1)}, u32[]{:S(2)}, u32[]{:S(2)}) collective-permute-start(f32[160,512]{1,0:T(8,128)} %copy-done.1), channel_id=1, source_target_pairs={{0,64},{32,96},{64,128},{96,160},{128,192},{160,224},{192,256},{22... | collective-permute-start | bytes 983048 | tf_op jit(solution)/shard_map/product/ppermute | solution.py:154
  77.7 4.1 %collective-permute-start.3 = (f32[96,512]{1,0:T(8,128)}, f32[96,512]{1,0:T(8,128)}, u32[]{:S(2)}, u32[]{:S(2)}) collective-permute-start(f32[96,512]{1,0:T(8,128)} %get-tuple-element.17), channel_id=1, source_target_pairs={{0,448},{32,480},{64,0},{96,32},{128,64},{160,96},{192,128},{224,1... | collective-permute-start | bytes 589832 | tf_op jit(solution)/shard_map/product/ppermute | solution.py:154
  81.8 0.0 all-to-all-done.3
  81.8 9.2 %inverse_factor.1.inv_ref = f32[256,256]{1,0:T(8,128)S(1)} custom-call(f32[256,256]{1,0:T(8,128)S(1)} %bitcast.16), custom_call_target="tpu_custom_call" | custom-call | flops 1000000000 | bytes 1048576 | tf_op jit(solution)/shard_map/factor/inverse_factor/pallas_call | solution.py:81
  91.0 0.0 collective-permute-done.left_ref
  91.0 0.0 collective-permute-done.1.right_ref
  91.0 0.8 collective-permute-done.3.down_ref
  91.8 1.1 collective-permute-done.2.up_ref
  92.9 1.6 %apply_inverse.1 = f32[256,512]{1,0:T(8,128)S(1)} custom-call(f32[256,256]{1,0:T(8,128)S(1)} %inverse_factor.1.inv_ref, f32[256,512]{1,0:T(8,128)S(1)} %get-tuple-element.13.mine_ref, f32[256,512]{1,0:T(8,128)S(1)} %collective-permute-done.left_ref, f32[256,512]{1,0:T(8,128)S(1)} %collective-permute-done.1.right_ref, ...), custom_call_target="tpu_custom_call" | custom-call | flops 600000000 | bytes 3145728 | tf_op jit(solution)/shard_map/projected/apply_inverse/pallas_call | solution.py:99
  94.5 0.7 convert_element_type.32
  95.3 10.4 %all-to-all-start.4 = ((f16[16,16,512]{2,1,0:T(8,128)(2,1)}), f16[16,16,512]{2,1,0:T(8,128)(2,1)S(1)}, u32[]{:S(2)}, u32[]{:S(2)}) async-start(f16[16,16,512]{2,1,0:T(8,128)(2,1)} %bitcast.4), calls=%async_computation.4 | async-start | bytes 524288 | tf_op jit(solution)/shard_map/projected/all_to_all | solution.py:192
  105.7 0.9 fusion.1
  106.7 17.5 %all-to-all-done.4 = f16[16,16,512]{2,1,0:T(8,128)(2,1)S(1)} async-done(((f16[16,16,512]{2,1,0:T(8,128)(2,1)}), f16[16,16,512]{2,1,0:T(8,128)(2,1)S(1)}, u32[]{:S(2)}, u32[]{:S(2)}) %all-to-all-start.4) | async-done | bytes 262176 | tf_op jit(solution)/shard_map/projected/all_to_all | solution.py:192
  124.2 0.7 copy.13
  (5 shorter events, 0.1 us)
Async XLA Ops:
  0.6 1.2 copy-start
  22.3 13.8 %all-to-all-start.1 = ((f16[32,24,256]{2,1,0:T(8,128)(2,1)}), f16[32,24,256]{2,1,0:T(8,128)(2,1)S(1)}, u32[]{:S(2)}, u32[]{:S(2)}) async-start(f16[32,24,256]{2,1,0:T(8,128)(2,1)} %broadcast_in_dim.6), calls=%async_computation.1 | async-start | bytes 786432 | tf_op jit(solution)/shard_map/sample/all_to_all | solution.py:173
  38.3 28.0 %all-to-all-start.2 = ((f32[16,8,256]{2,1,0:T(8,128)}), f32[16,8,256]{2,1,0:T(8,128)S(1)}, u32[]{:S(2)}, u32[]{:S(2)}) async-start(f32[16,8,256]{2,1,0:T(8,128)} %broadcast_in_dim.7), calls=%async_computation.2 | async-start | bytes 262144 | tf_op jit(solution)/shard_map/gram/all_to_all | solution.py:178
  57.1 0.7 copy-start.1
  57.8 33.2 %collective-permute-start = (f32[256,512]{1,0:T(8,128)}, f32[256,512]{1,0:T(8,128)S(1)}, u32[]{:S(2)}, u32[]{:S(2)}) collective-permute-start(f32[256,512]{1,0:T(8,128)} %get-tuple-element.14), channel_id=1, source_target_pairs={{0,32},{32,64},{64,96},{96,128},{128,160},{160,192},{192,224},{224... | collective-permute-start | bytes 1572872 | tf_op jit(solution)/shard_map/product/ppermute | solution.py:154
  61.6 29.3 %collective-permute-start.1 = (f32[256,512]{1,0:T(8,128)}, f32[256,512]{1,0:T(8,128)S(1)}, u32[]{:S(2)}, u32[]{:S(2)}) collective-permute-start(f32[256,512]{1,0:T(8,128)} %get-tuple-element.15), channel_id=1, source_target_pairs={{0,480},{32,0},{64,32},{96,64},{128,96},{160,128},{192,160},{224,1... | collective-permute-start | bytes 1572872 | tf_op jit(solution)/shard_map/product/ppermute | solution.py:154
  67.1 14.7 %all-to-all-start.3 = ((f32[32,8,256]{2,1,0:T(8,128)}), f32[32,8,256]{2,1,0:T(8,128)S(1)}, u32[]{:S(2)}, u32[]{:S(2)}) async-start(f32[32,8,256]{2,1,0:T(8,128)} %broadcast_in_dim.8), calls=%async_computation.3 | async-start | bytes 524288 | tf_op jit(solution)/shard_map/gram/all_to_all | solution.py:185
  73.6 19.3 %collective-permute-start.2 = (f32[160,512]{1,0:T(8,128)}, f32[160,512]{1,0:T(8,128)S(1)}, u32[]{:S(2)}, u32[]{:S(2)}) collective-permute-start(f32[160,512]{1,0:T(8,128)} %copy-done.1), channel_id=1, source_target_pairs={{0,64},{32,96},{64,128},{96,160},{128,192},{160,224},{192,256},{22... | collective-permute-start | bytes 983048 | tf_op jit(solution)/shard_map/product/ppermute | solution.py:154
  77.7 14.1 %collective-permute-start.3 = (f32[96,512]{1,0:T(8,128)}, f32[96,512]{1,0:T(8,128)}, u32[]{:S(2)}, u32[]{:S(2)}) collective-permute-start(f32[96,512]{1,0:T(8,128)} %get-tuple-element.17), channel_id=1, source_target_pairs={{0,448},{32,480},{64,0},{96,32},{128,64},{160,96},{192,128},{224,1... | collective-permute-start | bytes 589832 | tf_op jit(solution)/shard_map/product/ppermute | solution.py:154
  95.3 28.8 %all-to-all-start.4 = ((f16[16,16,512]{2,1,0:T(8,128)(2,1)}), f16[16,16,512]{2,1,0:T(8,128)(2,1)S(1)}, u32[]{:S(2)}, u32[]{:S(2)}) async-start(f16[16,16,512]{2,1,0:T(8,128)(2,1)} %bitcast.4), calls=%async_computation.4 | async-start | bytes 524288 | tf_op jit(solution)/shard_map/projected/all_to_all | solution.py:192
